TPU v7x, 256 devices: a whole 4x4x8 slice. The times are simulated.
256 devices in a mesh: doc: 4 (over x), ctx: 64 (over z, y, core).
Axes of the slice: x: 4, y: 4, z: 8, core: 2. Of those that a mesh axis runs over, the one named last changes fastest.
Arguments:
- query_vectors: bfloat16 [32768, 1024], P(('doc', 'ctx')), parts along dimension 0, may hold values from -8 to 8
- key_vectors: bfloat16 [32768, 1024], P(('doc', 'ctx')), parts along dimension 0, may hold values from -8 to 8
- value_vectors: bfloat16 [32768, 1024], P(('doc', 'ctx')), parts along dimension 0, may hold values from -8 to 8
Outputs:
- attended: bfloat16 [32768, 1024], P(('doc', 'ctx')), parts along dimension 0
There are 4 independent parts, one for each index of `doc`. A program takes and returns all parts, laid end to end along the dimension named above; each array names one. Nothing has to cross between parts.
All inputs are finite; a program needn't handle non-finite values.
Results may differ from a plain program's by a relative error of at most 0.0087.
The roundings to bfloat16 on the way count: a program that leaves them out, or rounds other values in their place, can miss the bound.
Values may be sent and summed in bfloat16 or wider, within the bound.
A program may use at most 64 MiB of HBM per device.

v0:
```python
import jax
import jax.numpy as jnp
from jax import lax
from jax.sharding import PartitionSpec as P

HEADS = 8
BLOCK = 128


masked_score = -1e30


def extended(cells, sides, width):
    for axis, dim in sides:
        count = lax.axis_size(axis)
        ends = count - 1
        head = lax.slice_in_dim(cells, 0, width, axis=dim)
        tail = lax.slice_in_dim(cells, cells.shape[dim] - width, cells.shape[dim], axis=dim)
        cells = jnp.concatenate(
            [
                lax.ppermute(tail, axis, [(i, (i + 1) % count) for i in range(ends)]),
                cells,
                lax.ppermute(head, axis, [((i + 1) % count, i) for i in range(ends)]),
            ],
            axis=dim,
        )
    return cells


def swapped(shard, axis, bit):
    return lax.ppermute(shard, axis, [(i, i ^ 1 << bit) for i in range(lax.axis_size(axis))])


def passed_along(shard, axis, by):
    length = lax.axis_size(axis)
    pairs = [(i, i + by) for i in range(length) if 0 <= i + by < length]
    return lax.ppermute(shard, axis, pairs)


def halve(rows):
    shape = rows.shape
    paired = rows.astype(jnp.float32).reshape(shape[:-2] + (shape[-2] // 2, 2, shape[-1]))
    return ((paired[..., 0, :] + paired[..., 1, :]) * 0.5).astype(jnp.bfloat16)


def attend(query_box, key_box, value_box, allowed, weight):
    boxes, query_count, width = query_box.shape
    key_count = key_box.shape[1]
    head_size = width // HEADS
    query_heads = query_box.reshape(boxes, query_count, HEADS, head_size)
    key_heads = key_box.reshape(boxes, key_count, HEADS, head_size)
    value_heads = value_box.reshape(boxes, key_count, HEADS, head_size)
    scores = jnp.einsum(
        "bqhd,bkhd->bhqk", query_heads, key_heads, preferred_element_type=jnp.float32
    ) * head_size ** (-0.5)
    scores = jnp.where(allowed[:, None, None, :], scores, masked_score)
    largest = jnp.max(scores, axis=-1)
    shifted = jnp.exp(scores - largest[..., None])
    totals = weight * jnp.sum(shifted, axis=-1)
    numerators = weight * jnp.einsum(
        "bhqk,bkhd->bqhd",
        shifted.astype(jnp.bfloat16),
        value_heads,
        preferred_element_type=jnp.float32,
    )
    largest = largest.transpose(0, 2, 1).reshape(boxes * query_count, HEADS)
    totals = totals.transpose(0, 2, 1).reshape(boxes * query_count, HEADS)
    return (largest, totals, numerators.reshape(boxes * query_count, HEADS, head_size))


def combine_level(running, terms, factor):
    largest, totals, numerators = terms
    largest = jnp.repeat(largest, factor, axis=0)
    totals = jnp.repeat(totals, factor, axis=0)
    numerators = jnp.repeat(numerators, factor, axis=0)
    run_peak, run_total, run_numer = running
    newest = jnp.maximum(run_peak, largest)
    keep_old = jnp.exp(run_peak - newest)
    keep_new = jnp.exp(largest - newest)
    return (
        newest,
        run_total * keep_old + totals * keep_new,
        run_numer * keep_old[..., None] + numerators * keep_new[..., None],
    )


def body(query_vectors, key_vectors, value_vectors):
    local_rows, width = query_vectors.shape
    devices = lax.axis_size("ctx")
    position = lax.axis_index("ctx")
    leaf_count = local_rows // BLOCK
    leaf_bits = leaf_count.bit_length() - 1
    device_bits = devices.bit_length() - 1
    summit = leaf_bits + device_bits - 2
    stacked = jnp.stack([key_vectors, value_vectors])
    padded = extended(stacked, (("ctx", 1),), BLOCK)
    neighbours = jnp.concatenate(
        [
            padded[:, shift_no * BLOCK : shift_no * BLOCK + local_rows].reshape(
                2, leaf_count, BLOCK, width
            )
            for shift_no in range(3)
        ],
        axis=2,
    )
    leaf_numbers = position * leaf_count + jnp.arange(leaf_count, dtype=jnp.int32)
    total_leaves = leaf_count * devices
    allowed = jnp.concatenate(
        [
            jnp.broadcast_to((leaf_numbers >= 1)[:, None], (leaf_count, BLOCK)),
            jnp.ones((leaf_count, BLOCK), dtype=bool),
            jnp.broadcast_to((leaf_numbers < total_leaves - 1)[:, None], (leaf_count, BLOCK)),
        ],
        axis=1,
    )
    running = attend(
        query_vectors.reshape(leaf_count, BLOCK, width), neighbours[0], neighbours[1], allowed, 1.0
    )
    coarse_query, coarse_key, coarse_value = (query_vectors, key_vectors, value_vectors)
    first_gathered = summit + 1
    owned_pair = jnp.stack([coarse_key, coarse_value])
    query_box = coarse_query
    for height in range(leaf_bits, first_gathered):
        bit_place = height - leaf_bits
        partner = swapped(owned_pair, "ctx", bit_place)
        upper_half = position >> bit_place & 1
        lower_first = jnp.where(upper_half == 1, partner, owned_pair)
        higher = jnp.where(upper_half == 1, owned_pair, partner)
        family = jnp.concatenate([lower_first, higher], axis=1)
        if height >= 1:
            distance = 2 << bit_place
            arrived = [passed_along(family, "ctx", moved) for moved in (distance, -distance)]
            left_family, right_family = arrived
            parent = position >> bit_place >> 1
            parents_total = devices >> bit_place + 1
            left_valid = parent >= 1
            right_valid = parent + 1 < parents_total
            even_box = upper_half == 0
            middle = jnp.where(even_box, right_family[:, :BLOCK], left_family[:, BLOCK:])
            middle_valid = jnp.where(even_box, right_valid, left_valid)
            candidates = jnp.concatenate(
                [left_family[:, :BLOCK], middle, right_family[:, BLOCK:]], axis=1
            )[:, None]
            allowed = jnp.concatenate(
                [
                    jnp.broadcast_to(left_valid, (1, BLOCK)),
                    jnp.broadcast_to(middle_valid, (1, BLOCK)),
                    jnp.broadcast_to(right_valid, (1, BLOCK)),
                ],
                axis=1,
            )
            terms = attend(query_box[None], candidates[0], candidates[1], allowed, float(2**height))
            running = combine_level(running, terms, 2**height)
        owned_pair = halve(family)
        if height < summit:
            query_box = halve(query_box)
    run_peak, run_total, run_numer = running
    return (run_numer / run_total[..., None]).reshape(local_rows, width).astype(jnp.bfloat16)


def solution(mesh):
    return jax.shard_map(
        body,
        mesh=mesh,
        in_specs=(P(("doc", "ctx"), None), P(("doc", "ctx"), None), P(("doc", "ctx"), None)),
        out_specs=P(("doc", "ctx"), None),
        check_vma=False,
    )
```

profile of v0, /device:TPU:252, one launch (start us, length us, event | category | flops | bytes accessed | tf_op | source)
XLA Modules:
  0.0 241.1 jit_solution(14268677576311393246)
XLA Ops:
  0.0 1.2 copy.252
  1.2 1.1 copy.253
  2.3 0.8 pad_maximum_fusion.9
  3.2 2.8 %collective-permute-start.1 = (bf16[2,128,1024]{1,2,0:T(8,128)(2,1)}, bf16[2,128,1024]{1,2,0:T(8,128)(2,1)}, u32[]{:S(2)}, u32[]{:S(2)}) collective-permute-start(bf16[2,128,1024]{1,2,0:T(8,128)(2,1)} %pad_maximum_fusion.9), channel_id=1, source_target_pairs={{1,0},{2,1},{3,2},{4,3},{5,4},{6,5},{7,6},{8,7},{9,8},{10,9},{11,1... | collective-permute-start | bytes 1572872 | tf_op jit(solution)/shard_map/ppermute | solution.py:23
  5.9 2.4 collective-permute-start
  9.5 1.5 maximum_convert_fusion
  10.9 2.9 %copy.261 = f32[2,256,1024]{2,0,1:T(2,128)S(1)} copy(f32[2,256,1024]{1,2,0:T(8,128)} %maximum_convert_fusion) | data formatting | bytes 4194304 | tf_op jit(solution)/shard_map/convert_element_type | solution.py:42
  13.9 0.8 fusion.88
  14.6 0.6 fusion.24
  15.3 1.1 convert_reduce_fusion.1
  17.4 0.8 convert_reduce_fusion.3
  18.4 0.5 fusion.62
  19.0 0.5 fusion.61
  19.5 0.6 fusion.60
  20.1 9.0 %collective-permute-done.3 = bf16[2,128,1024]{2,1,0:T(8,128)(2,1)S(1)} collective-permute-done((bf16[2,128,1024]{2,1,0:T(8,128)(2,1)S(1)}, bf16[2,128,1024]{2,1,0:T(8,128)(2,1)S(1)}, u32[]{:S(2)}, u32[]{:S(2)}) %collective-permute-start.3) | collective-permute-done | bytes 524320 | tf_op jit(solution)/shard_map/ppermute | solution.py:31
  29.2 1.3 pad_maximum_fusion.5
  30.5 1.6 copy.276
  32.2 0.8 fusion.87
  32.9 0.6 fusion.25
  33.5 2.3 collective-permute-start.6
  35.8 0.7 convert_reduce_fusion.4
  36.6 1.4 pad_maximum_fusion
  38.1 4.3 %collective-permute-start.5 = (bf16[2,256,1024]{2,1,0:T(8,128)(2,1)}, bf16[2,256,1024]{2,1,0:T(8,128)(2,1)}, u32[]{:S(2)}, u32[]{:S(2)}) collective-permute-start(bf16[2,256,1024]{2,1,0:T(8,128)(2,1)} %get-tuple-element.39), channel_id=1, source_target_pairs={{4,0},{5,1},{6,2},{7,3},{8,4},{9,5},{10,6},{11,7},{12,8},{13,9},{1... | collective-permute-start | bytes 3145736 | tf_op jit(solution)/shard_map/ppermute | solution.py:37
  42.4 1.5 collective-permute-start.4
  43.9 26.8 %collective-permute-done.6 = bf16[2,128,1024]{2,1,0:T(8,128)(2,1)S(1)} collective-permute-done((bf16[2,128,1024]{2,1,0:T(8,128)(2,1)S(1)}, bf16[2,128,1024]{2,1,0:T(8,128)(2,1)S(1)}, u32[]{:S(2)}, u32[]{:S(2)}) %collective-permute-start.6) | collective-permute-done | bytes 524320 | tf_op jit(solution)/shard_map/ppermute | solution.py:31
  70.8 1.3 pad_maximum_fusion.6
  72.1 1.6 copy.290
  73.7 0.8 fusion.86
  74.5 0.6 fusion.26
  75.1 1.1 collective-permute-start.9
  76.2 0.5 bitcast_reduce_fusion
  77.6 3.9 %collective-permute-start.8 = (bf16[2,256,1024]{2,1,0:T(8,128)(2,1)}, bf16[2,256,1024]{2,1,0:T(8,128)(2,1)}, u32[]{:S(2)}, u32[]{:S(2)}) collective-permute-start(bf16[2,256,1024]{2,1,0:T(8,128)(2,1)} %get-tuple-element.44), channel_id=1, source_target_pairs={{8,0},{9,1},{10,2},{11,3},{12,4},{13,5},{14,6},{15,7},{16,8},{17,9... | collective-permute-start | bytes 3145736 | tf_op jit(solution)/shard_map/ppermute | solution.py:37
  81.5 1.3 collective-permute-start.7
  82.8 7.2 %collective-permute-done.9 = bf16[2,128,1024]{2,1,0:T(8,128)(2,1)} collective-permute-done((bf16[2,128,1024]{2,1,0:T(8,128)(2,1)S(1)}, bf16[2,128,1024]{2,1,0:T(8,128)(2,1)}, u32[]{:S(2)}, u32[]{:S(2)}) %collective-permute-start.9) | collective-permute-done | bytes 524320 | tf_op jit(solution)/shard_map/ppermute | solution.py:31
  90.0 1.1 broadcast_select_fusion.3
  91.1 1.4 pad_maximum_fusion.7
  92.5 4.1 %collective-permute-start.11 = (bf16[2,256,1024]{2,1,0:T(8,128)(2,1)}, bf16[2,256,1024]{2,1,0:T(8,128)(2,1)}, u32[]{:S(2)}, u32[]{:S(2)}) collective-permute-start(bf16[2,256,1024]{2,1,0:T(8,128)(2,1)} %get-tuple-element.49), channel_id=1, source_target_pairs={{16,0},{17,1},{18,2},{19,3},{20,4},{21,5},{22,6},{23,7},{24,8},{25... | collective-permute-start | bytes 3145736 | tf_op jit(solution)/shard_map/ppermute | solution.py:37
  96.6 1.3 collective-permute-start.10
  97.9 1.6 fusion.94
  99.6 1.3 fusion.91
  100.9 1.5 copy.271
  102.4 2.3 copy.264
  104.7 1.6 copy.301
  106.3 0.8 fusion.85
  107.1 0.6 fusion.27
  107.7 3.6 %collective-permute-start.12 = (bf16[2,128,1024]{2,1,0:T(8,128)(2,1)S(1)}, bf16[2,128,1024]{2,1,0:T(8,128)(2,1)}, u32[]{:S(2)}, u32[]{:S(2)}) collective-permute-start(bf16[2,128,1024]{2,1,0:T(8,128)(2,1)S(1)} %fusion.27), channel_id=1, source_target_pairs={{0,16},{1,17},{2,18},{3,19},{4,20},{5,21},{6,22},{7,23},{8,24},{9,... | collective-permute-start | bytes 1572872 | tf_op jit(solution)/shard_map/ppermute | solution.py:31
  111.7 0.5 fusion.5
  113.0 0.7 copy.268
  113.6 62.3 %collective-permute-done.12 = bf16[2,128,1024]{2,1,0:T(8,128)(2,1)} collective-permute-done((bf16[2,128,1024]{2,1,0:T(8,128)(2,1)S(1)}, bf16[2,128,1024]{2,1,0:T(8,128)(2,1)}, u32[]{:S(2)}, u32[]{:S(2)}) %collective-permute-start.12) | collective-permute-done | bytes 524320 | tf_op jit(solution)/shard_map/ppermute | solution.py:31
  175.9 1.1 broadcast_select_fusion.1
  177.0 1.1 pad_maximum_fusion.8
  178.1 3.2 %collective-permute-start.14 = (bf16[2,256,1024]{2,1,0:T(8,128)(2,1)}, bf16[2,256,1024]{2,1,0:T(8,128)(2,1)}, u32[]{:S(2)}, u32[]{:S(2)}) collective-permute-start(bf16[2,256,1024]{2,1,0:T(8,128)(2,1)} %pad_maximum_fusion.8), channel_id=1, source_target_pairs={{32,0},{33,1},{34,2},{35,3},{36,4},{37,5},{38,6},{39,7},{40,8},{41... | collective-permute-start | bytes 3145736 | tf_op jit(solution)/shard_map/ppermute | solution.py:37
  181.3 1.3 collective-permute-start.13
  182.6 1.6 fusion.95
  185.7 0.4 fusion.7
  186.6 0.7 copy.317
  187.3 0.7 copy.283
  188.0 1.6 fusion.96
  191.0 0.4 fusion.9
  191.5 0.7 reshape.621
  192.6 33.8 %collective-permute-done.14 = bf16[2,256,1024]{2,1,0:T(8,128)(2,1)} collective-permute-done((bf16[2,256,1024]{2,1,0:T(8,128)(2,1)}, bf16[2,256,1024]{2,1,0:T(8,128)(2,1)}, u32[]{:S(2)}, u32[]{:S(2)}) %collective-permute-start.14) | collective-permute-done | bytes 1048608 | tf_op jit(solution)/shard_map/ppermute | solution.py:37
  226.4 6.2 %collective-permute-done.13 = bf16[2,256,1024]{2,1,0:T(8,128)(2,1)} collective-permute-done((bf16[2,256,1024]{2,1,0:T(8,128)(2,1)}, bf16[2,256,1024]{2,1,0:T(8,128)(2,1)}, u32[]{:S(2)}, u32[]{:S(2)}) %collective-permute-start.13) | collective-permute-done | bytes 1048608 | tf_op jit(solution)/shard_map/ppermute | solution.py:37
  232.6 1.6 fusion.97
  239.5 1.7 fusion.28
  (151 shorter events, 13.2 us)
Async XLA Ops:
  0.0 8.3 %copy-start.1 = (bf16[128,1024]{1,0:T(8,128)(2,1)S(1)}, bf16[128,1024]{1,0:T(8,128)(2,1)}, u32[]{:S(2)}) copy-start(bf16[128,1024]{1,0:T(8,128)(2,1)} %param.3) | copy-start | bytes 786436
  3.1 6.2 %collective-permute-start.2 = (bf16[2,128,1024]{1,2,0:T(8,128)(2,1)}, bf16[2,128,1024]{1,2,0:T(8,128)(2,1)S(1)}, u32[]{:S(2)}, u32[]{:S(2)}) collective-permute-start(bf16[2,128,1024]{1,2,0:T(8,128)(2,1)} %pad_maximum_fusion.9), channel_id=1, source_target_pairs={{0,1},{1,0},{2,3},{3,2},{4,5},{5,4},{6,7},{7,6},{8,9},{9,8},{10,11... | collective-permute-start | bytes 1572872 | tf_op jit(solution)/shard_map/ppermute | solution.py:31
  3.2 33.4 %collective-permute-start.1 = (bf16[2,128,1024]{1,2,0:T(8,128)(2,1)}, bf16[2,128,1024]{1,2,0:T(8,128)(2,1)}, u32[]{:S(2)}, u32[]{:S(2)}) collective-permute-start(bf16[2,128,1024]{1,2,0:T(8,128)(2,1)} %pad_maximum_fusion.9), channel_id=1, source_target_pairs={{1,0},{2,1},{3,2},{4,3},{5,4},{6,5},{7,6},{8,7},{9,8},{10,9},{11,1... | collective-permute-start | bytes 1572872 | tf_op jit(solution)/shard_map/ppermute | solution.py:23
  5.9 30.6 %collective-permute-start = (bf16[2,128,1024]{1,2,0:T(8,128)(2,1)}, bf16[2,128,1024]{1,2,0:T(8,128)(2,1)}, u32[]{:S(2)}, u32[]{:S(2)}) collective-permute-start(bf16[2,128,1024]{1,2,0:T(8,128)(2,1)} %pad_maximum_fusion.9), channel_id=1, source_target_pairs={{0,1},{1,2},{2,3},{3,4},{4,5},{5,6},{6,7},{7,8},{8,9},{9,10},{10,1... | collective-permute-start | bytes 1572872 | tf_op jit(solution)/shard_map/ppermute | solution.py:21
  15.2 13.9 %collective-permute-start.3 = (bf16[2,128,1024]{2,1,0:T(8,128)(2,1)S(1)}, bf16[2,128,1024]{2,1,0:T(8,128)(2,1)S(1)}, u32[]{:S(2)}, u32[]{:S(2)}) collective-permute-start(bf16[2,128,1024]{2,1,0:T(8,128)(2,1)S(1)} %fusion.24), channel_id=1, source_target_pairs={{0,2},{1,3},{2,0},{3,1},{4,6},{5,7},{6,4},{7,5},{8,10},{9,11},{10,... | collective-permute-start | bytes 1572872 | tf_op jit(solution)/shard_map/ppermute | solution.py:31
  33.5 37.2 %collective-permute-start.6 = (bf16[2,128,1024]{2,1,0:T(8,128)(2,1)S(1)}, bf16[2,128,1024]{2,1,0:T(8,128)(2,1)S(1)}, u32[]{:S(2)}, u32[]{:S(2)}) collective-permute-start(bf16[2,128,1024]{2,1,0:T(8,128)(2,1)S(1)} %fusion.25), channel_id=1, source_target_pairs={{0,4},{1,5},{2,6},{3,7},{4,0},{5,1},{6,2},{7,3},{8,12},{9,13},{10,... | collective-permute-start | bytes 1572872 | tf_op jit(solution)/shard_map/ppermute | solution.py:31
  38.1 58.4 %collective-permute-start.5 = (bf16[2,256,1024]{2,1,0:T(8,128)(2,1)}, bf16[2,256,1024]{2,1,0:T(8,128)(2,1)}, u32[]{:S(2)}, u32[]{:S(2)}) collective-permute-start(bf16[2,256,1024]{2,1,0:T(8,128)(2,1)} %get-tuple-element.39), channel_id=1, source_target_pairs={{4,0},{5,1},{6,2},{7,3},{8,4},{9,5},{10,6},{11,7},{12,8},{13,9},{1... | collective-permute-start | bytes 3145736 | tf_op jit(solution)/shard_map/ppermute | solution.py:37
  42.4 55.4 %collective-permute-start.4 = (bf16[2,256,1024]{2,1,0:T(8,128)(2,1)}, bf16[2,256,1024]{2,1,0:T(8,128)(2,1)}, u32[]{:S(2)}, u32[]{:S(2)}) collective-permute-start(bf16[2,256,1024]{2,1,0:T(8,128)(2,1)} %get-tuple-element.39), channel_id=1, source_target_pairs={{0,4},{1,5},{2,6},{3,7},{4,8},{5,9},{6,10},{7,11},{8,12},{9,13},{1... | collective-permute-start | bytes 3145736 | tf_op jit(solution)/shard_map/ppermute | solution.py:37
  75.1 14.9 %collective-permute-start.9 = (bf16[2,128,1024]{2,1,0:T(8,128)(2,1)S(1)}, bf16[2,128,1024]{2,1,0:T(8,128)(2,1)}, u32[]{:S(2)}, u32[]{:S(2)}) collective-permute-start(bf16[2,128,1024]{2,1,0:T(8,128)(2,1)S(1)} %fusion.26), channel_id=1, source_target_pairs={{0,8},{1,9},{2,10},{3,11},{4,12},{5,13},{6,14},{7,15},{8,0},{9,1},... | collective-permute-start | bytes 1572872 | tf_op jit(solution)/shard_map/ppermute | solution.py:31
  77.6 103.8 %collective-permute-start.8 = (bf16[2,256,1024]{2,1,0:T(8,128)(2,1)}, bf16[2,256,1024]{2,1,0:T(8,128)(2,1)}, u32[]{:S(2)}, u32[]{:S(2)}) collective-permute-start(bf16[2,256,1024]{2,1,0:T(8,128)(2,1)} %get-tuple-element.44), channel_id=1, source_target_pairs={{8,0},{9,1},{10,2},{11,3},{12,4},{13,5},{14,6},{15,7},{16,8},{17,9... | collective-permute-start | bytes 3145736 | tf_op jit(solution)/shard_map/ppermute | solution.py:37
  81.5 101.1 %collective-permute-start.7 = (bf16[2,256,1024]{2,1,0:T(8,128)(2,1)}, bf16[2,256,1024]{2,1,0:T(8,128)(2,1)}, u32[]{:S(2)}, u32[]{:S(2)}) collective-permute-start(bf16[2,256,1024]{2,1,0:T(8,128)(2,1)} %get-tuple-element.44), channel_id=1, source_target_pairs={{0,8},{1,9},{2,10},{3,11},{4,12},{5,13},{6,14},{7,15},{8,16},{9,17... | collective-permute-start | bytes 3145736 | tf_op jit(solution)/shard_map/ppermute | solution.py:37
  92.5 95.5 %collective-permute-start.11 = (bf16[2,256,1024]{2,1,0:T(8,128)(2,1)}, bf16[2,256,1024]{2,1,0:T(8,128)(2,1)}, u32[]{:S(2)}, u32[]{:S(2)}) collective-permute-start(bf16[2,256,1024]{2,1,0:T(8,128)(2,1)} %get-tuple-element.49), channel_id=1, source_target_pairs={{16,0},{17,1},{18,2},{19,3},{20,4},{21,5},{22,6},{23,7},{24,8},{25... | collective-permute-start | bytes 3145736 | tf_op jit(solution)/shard_map/ppermute | solution.py:37
  96.6 91.4 %collective-permute-start.10 = (bf16[2,256,1024]{2,1,0:T(8,128)(2,1)}, bf16[2,256,1024]{2,1,0:T(8,128)(2,1)}, u32[]{:S(2)}, u32[]{:S(2)}) collective-permute-start(bf16[2,256,1024]{2,1,0:T(8,128)(2,1)} %get-tuple-element.49), channel_id=1, source_target_pairs={{0,16},{1,17},{2,18},{3,19},{4,20},{5,21},{6,22},{7,23},{8,24},{9,... | collective-permute-start | bytes 3145736 | tf_op jit(solution)/shard_map/ppermute | solution.py:37
  107.1 4.3 %copy-start = (bf16[1,384,1024]{1,2,0:T(8,128)(2,1)S(1)}, bf16[1,384,1024]{1,2,0:T(8,128)(2,1)}, u32[]{:S(2)}) copy-start(bf16[1,384,1024]{1,2,0:T(8,128)(2,1)} %copy.264) | copy-start | bytes 2359300
  107.7 68.2 %collective-permute-start.12 = (bf16[2,128,1024]{2,1,0:T(8,128)(2,1)S(1)}, bf16[2,128,1024]{2,1,0:T(8,128)(2,1)}, u32[]{:S(2)}, u32[]{:S(2)}) collective-permute-start(bf16[2,128,1024]{2,1,0:T(8,128)(2,1)S(1)} %fusion.27), channel_id=1, source_target_pairs={{0,16},{1,17},{2,18},{3,19},{4,20},{5,21},{6,22},{7,23},{8,24},{9,... | collective-permute-start | bytes 1572872 | tf_op jit(solution)/shard_map/ppermute | solution.py:31
  178.1 48.3 %collective-permute-start.14 = (bf16[2,256,1024]{2,1,0:T(8,128)(2,1)}, bf16[2,256,1024]{2,1,0:T(8,128)(2,1)}, u32[]{:S(2)}, u32[]{:S(2)}) collective-permute-start(bf16[2,256,1024]{2,1,0:T(8,128)(2,1)} %pad_maximum_fusion.8), channel_id=1, source_target_pairs={{32,0},{33,1},{34,2},{35,3},{36,4},{37,5},{38,6},{39,7},{40,8},{41... | collective-permute-start | bytes 3145736 | tf_op jit(solution)/shard_map/ppermute | solution.py:37
  181.3 51.3 %collective-permute-start.13 = (bf16[2,256,1024]{2,1,0:T(8,128)(2,1)}, bf16[2,256,1024]{2,1,0:T(8,128)(2,1)}, u32[]{:S(2)}, u32[]{:S(2)}) collective-permute-start(bf16[2,256,1024]{2,1,0:T(8,128)(2,1)} %pad_maximum_fusion.8), channel_id=1, source_target_pairs={{0,32},{1,33},{2,34},{3,35},{4,36},{5,37},{6,38},{7,39},{8,40},{9,... | collective-permute-start | bytes 3145736 | tf_op jit(solution)/shard_map/ppermute | solution.py:37
  184.5 0.8 copy-start.2
  184.6 0.8 copy-start.11
  189.9 0.8 copy-start.3
  189.9 0.8 copy-start.9
  234.5 0.8 copy-start.4
  234.5 0.8 copy-start.10
  234.9 1.7 copy-start.5
  234.9 1.7 copy-start.6
  234.9 1.7 copy-start.7
  234.9 1.7 copy-start.8
where the time goes:
time: 242 us; the launch traced here: 241 us
  waiting for transfers between devices  145 us (60%)
  starting transfers between devices  33.1 us (14%)
  local copies, waits for them, and re-layouts  29.2 us (12%)
  other arithmetic  28.6 us (12%)
  matrix products  4.05 us (2%)
    ppermute x5, waiting for transfers between devices, swapped(): lax.ppermute(shard, axis, [(i, i ^ 1 << bit) for i in range(lax.axis_size...  105 us
    ppermute x8, waiting for transfers between devices, passed_along(): return lax.ppermute(shard, axis, pairs)  40 us
    ppermute x8, starting transfers between devices, passed_along(): return lax.ppermute(shard, axis, pairs)  20.8 us
    convert_element_type x7, local copies, waits for them, and re-layouts, halve(): rows.astype(jnp.float32)  8.07 us
    ppermute x5, starting transfers between devices, swapped(): lax.ppermute(shard, axis, [(i, i ^ 1 << bit) for i in range(lax.axis_size...  7.14 us
    slice x4, other arithmetic, body(): left_family[:, :BLOCK]  6.57 us
    convert_element_type x8, other arithmetic, halve(): return ((paired[..., 0, :] + paired[..., 1, :]) * 0.5).astype(jnp.bfloat16)  5.17 us
    concatenate x4, other arithmetic, body(): family = jnp.concatenate([lower_first, higher], axis=1)  5.11 us
  transfers between devices with their start and end apart: 15, of which 6 were waited for; matrix products, arithmetic and copies ran while one was open for 21% of the time, Pallas kernels for 0%

commit v1 on v0

v1 whole, which is shorter than its diff:
```python
import functools
import math

import jax
import jax.numpy as jnp
from jax import lax
from jax.experimental import pallas as pl
from jax.experimental.pallas import tpu as pltpu
from jax.sharding import PartitionSpec as P

MESH = pl.DeviceIdType.MESH
HEADS = 8
BOX = 128
ROWS = 8
MASKED = -1e30
TO_LOG2 = math.log2(math.e) / math.sqrt(128.0)


def pool(rows):
    count = rows.shape[0]
    target = lax.broadcasted_iota(jnp.int32, (count // 2, count), 0)
    source = lax.broadcasted_iota(jnp.int32, (count // 2, count), 1)
    pairs = jnp.where(source // 2 == target, 0.5, 0.0).astype(jnp.bfloat16)
    return jnp.dot(pairs, rows, preferred_element_type=jnp.float32).astype(jnp.bfloat16)


def attend(query, keys, values, biases):
    scores = []
    for key, bias in zip(keys, biases):
        score = lax.dot_general(query, key, (((1,), (1,)), ((), ())), preferred_element_type=jnp.float32) * TO_LOG2
        scores.append(score if bias is None else score + bias)
    peak = jnp.max(functools.reduce(jnp.maximum, scores), axis=1, keepdims=True)
    shifted = [jnp.exp2(score - peak) for score in scores]
    total = jnp.sum(functools.reduce(jnp.add, shifted), axis=1, keepdims=True)
    weights = jnp.concatenate([part.astype(jnp.bfloat16) for part in shifted], axis=1)
    numerator = jnp.dot(weights, jnp.concatenate(values, axis=0), preferred_element_type=jnp.float32)
    return jnp.broadcast_to(peak, numerator.shape), jnp.broadcast_to(total, numerator.shape), numerator


def merge(one, other):
    newest = jnp.maximum(one[0], other[0])
    keep_one = jnp.exp2(one[0] - newest)
    keep_other = jnp.exp2(other[0] - newest)
    return newest, one[1] * keep_one + other[1] * keep_other, one[2] * keep_one + other[2] * keep_other


def kernel(zs, q_hbm, k_hbm, v_hbm, out_ref, source, q0, q1, q2, kv0, kv1, kv2, kv3, kv4, terms0, terms1, spread, done, load_sem, send_sem, recv_sem):
    me = lax.axis_index("ctx")
    z = me // ROWS
    rank = lax.rem(me, ROWS)
    odd = lax.rem(z, 2)

    def ring(step):
        return z * ROWS + lax.rem(rank + step, ROWS)

    def column(other):
        return lax.rem(other + zs, zs) * ROWS + rank

    def mate(other):
        return other + 1 - 2 * lax.rem(other, 2)

    opposite = lax.rem(z + zs // 2, zs)
    mirrored = zs - 1 - z
    has_left = z > 0
    has_right = z < zs - 1
    has_a = z >= 2
    has_b = z < zs - 2
    has_c = ((odd == 0) & (z + 3 < zs)) | ((odd == 1) & (z >= 3))
    has_e = (z < 2) | (z >= zs - 2)
    third = z + 3 - 6 * odd

    loads = [
        pltpu.make_async_copy(ref, source.at[n], load_sem.at[n]) for n, ref in enumerate((k_hbm, v_hbm, q_hbm))
    ]
    for load in loads:
        load.start()
    barrier = pltpu.get_barrier_semaphore()
    for step in range(1, ROWS):
        pl.semaphore_signal(barrier, inc=1, device_id={"ctx": ring(step)}, device_id_type=MESH)
    for step in range(1, zs):
        pl.semaphore_signal(barrier, inc=1, device_id={"ctx": column(z + step)}, device_id_type=MESH)

    def blank(ref, present, start, count):
        @pl.when(jnp.logical_not(present))
        def _():
            ref[:, start : start + count, :] = jnp.zeros((2, count, BOX), jnp.bfloat16)

    blank(kv0, has_left, 0, BOX)
    blank(kv0, has_right, 9 * BOX, BOX)
    blank(kv1, has_left, 0, 2 * BOX)
    blank(kv1, has_right, 6 * BOX, 2 * BOX)
    blank(kv2, has_left, 0, BOX)
    blank(kv2, has_right, 5 * BOX, BOX)
    blank(kv3, has_a, 0, BOX)
    blank(kv3, has_b, BOX, BOX)
    blank(kv3, has_c, 2 * BOX, BOX)
    blank(kv4, has_e, BOX, BOX)

    used = [0]

    def remote(src, dst, device):
        number = used[0]
        used[0] += 1
        return pltpu.make_async_remote_copy(
            src_ref=src,
            dst_ref=dst,
            send_sem=send_sem.at[number],
            recv_sem=recv_sem.at[number],
            device_id={"ctx": device},
            device_id_type=MESH,
        )

    def when(present, action):
        if present is None:
            action()
        else:
            pl.when(present)(action)

    sent = []

    def send(src, dst, device, goes=None, comes=None):
        copy = remote(src, dst, device)
        when(goes, copy.start)
        sent.append((copy, goes))
        return copy, comes

    def arrive(message):
        when(message[1], message[0].wait_recv)

    pl.semaphore_wait(barrier, ROWS - 1 + zs - 1)

    def head(number):
        return pl.ds(pl.multiple_of(number * BOX, BOX), BOX)

    loads[0].wait()
    loads[1].wait()
    kv_in = [
        send(
            source.at[pl.ds(0, 2), :, head(lax.rem(rank + step, ROWS))],
            kv0.at[:, head(rank + 1), :],
            ring(step),
        )
        for step in range(1, ROWS)
    ]
    own_kv = pltpu.make_async_copy(source.at[pl.ds(0, 2), :, head(rank)], kv0.at[:, head(rank + 1), :], load_sem.at[3])
    own_kv.start()
    loads[2].wait()
    q_in = [
        send(source.at[2, :, head(lax.rem(rank + step, ROWS))], q0.at[head(rank), :], ring(step))
        for step in range(1, ROWS)
    ]
    own_q = pltpu.make_async_copy(source.at[2, :, head(rank)], q0.at[head(rank), :], load_sem.at[4])
    own_q.start()

    own_kv.wait()
    for message in kv_in:
        arrive(message)

    def box(ref, kind, start):
        return ref[kind, start * BOX : (start + 1) * BOX, :]

    left0 = send(kv0.at[:, pl.ds(8 * BOX, BOX), :], kv0.at[:, pl.ds(0, BOX), :], column(z + 1), has_right, has_left)
    right0 = send(kv0.at[:, pl.ds(BOX, BOX), :], kv0.at[:, pl.ds(9 * BOX, BOX), :], column(z - 1), has_left, has_right)
    for kind in range(2):
        for n in range(4):
            kv1[kind, (2 + n) * BOX : (3 + n) * BOX, :] = pool(kv0[kind, (2 * n + 1) * BOX : (2 * n + 3) * BOX, :])
    for kind in range(2):
        for n in range(2):
            kv2[kind, (2 + n) * BOX : (3 + n) * BOX, :] = pool(kv1[kind, (2 * n + 2) * BOX : (2 * n + 4) * BOX, :])
        kv3[kind, 3 * BOX : 4 * BOX, :] = pool(kv2[kind, 2 * BOX : 4 * BOX, :])
        kv4[kind, 2 * BOX : 2 * BOX + BOX // 2, :] = pool(kv3[kind, 3 * BOX : 4 * BOX, :])

    own4 = kv4.at[:, pl.ds(2 * BOX, BOX // 2), :]
    half = pl.multiple_of(odd * (BOX // 2), BOX // 2)
    d_in = [
        send(own4, kv4.at[:, pl.ds(half, BOX // 2), :], column(opposite)),
        send(own4, kv4.at[:, pl.ds(half, BOX // 2), :], column(mate(opposite))),
    ]
    e_in = [
        send(own4, kv4.at[:, pl.ds(BOX + half, BOX // 2), :], column(mate(mirrored)), has_e, has_e),
        send(own4, kv4.at[:, pl.ds(BOX + half, BOX // 2), :], column(mirrored), has_e, has_e),
    ]
    own3 = kv3.at[:, pl.ds(3 * BOX, BOX), :]
    c_in = send(own3, kv3.at[:, pl.ds(2 * BOX, BOX), :], column(third), has_c, has_c)
    a_in = send(own3, kv3.at[:, pl.ds(0, BOX), :], column(z + 2), has_b, has_a)
    b_in = send(own3, kv3.at[:, pl.ds(BOX, BOX), :], column(z - 2), has_a, has_b)
    left1 = send(kv1.at[:, pl.ds(4 * BOX, 2 * BOX), :], kv1.at[:, pl.ds(0, 2 * BOX), :], column(z + 1), has_right, has_left)
    right1 = send(kv1.at[:, pl.ds(2 * BOX, 2 * BOX), :], kv1.at[:, pl.ds(6 * BOX, 2 * BOX), :], column(z - 1), has_left, has_right)
    left2 = send(kv2.at[:, pl.ds(2 * BOX, BOX), :], kv2.at[:, pl.ds(0, BOX), :], column(z + 1), has_right, has_left)
    right2 = send(kv2.at[:, pl.ds(3 * BOX, BOX), :], kv2.at[:, pl.ds(5 * BOX, BOX), :], column(z - 1), has_left, has_right)

    def bias(present):
        return jnp.where(present, 0.0, MASKED).astype(jnp.float32)

    left_bias, right_bias = bias(has_left), bias(has_right)

    own_q.wait()
    for message in q_in:
        arrive(message)
    for n in range(4):
        q1[n * BOX : (n + 1) * BOX, :] = pool(q0[2 * n * BOX : (2 * n + 2) * BOX, :])
    for n in range(2):
        q2[n * BOX : (n + 1) * BOX, :] = pool(q1[2 * n * BOX : (2 * n + 2) * BOX, :])
    q3 = pool(q2[...])
    q4 = pool(q3)

    def level(query, ref, boxes, biases):
        return attend(query, [box(ref, 0, b) for b in boxes], [box(ref, 1, b) for b in boxes], biases)

    def keep(ref, n, values):
        for kind in range(3):
            ref[kind, n * BOX : (n + 1) * BOX, :] = values[kind]

    def kept(ref, n):
        return tuple(ref[kind, n * BOX : (n + 1) * BOX, :] for kind in range(3))

    def level0(n):
        biases = [left_bias if n == 0 else None, None, right_bias if n == ROWS - 1 else None]
        keep(terms0, n, level(q0[n * BOX : (n + 1) * BOX, :], kv0, (n, n + 1, n + 2), biases))

    for n in range(1, ROWS - 1):
        level0(n)
    arrive(left0)
    arrive(right0)
    level0(0)
    level0(ROWS - 1)

    def raised(values, height):
        return values[0] + float(height), values[1], values[2]

    arrive(left1)
    arrive(right1)
    for n, boxes in enumerate(((0, 4, 5), (1, 5, 0), (2, 6, 7), (3, 7, 2))):
        biases = [left_bias if b < 2 else right_bias if b >= 6 else None for b in boxes]
        keep(terms1, n, raised(level(q1[n * BOX : (n + 1) * BOX, :], kv1, boxes, biases), 1))
    for kind in range(2):
        kv2[kind, BOX : 2 * BOX, :] = pool(kv1[kind, 0 : 2 * BOX, :])
        kv2[kind, 4 * BOX : 5 * BOX, :] = pool(kv1[kind, 6 * BOX : 8 * BOX, :])
    arrive(left2)
    arrive(right2)

    def doubled(values, slot):
        count = values[0].shape[0]
        for kind in range(3):
            spread[slot, kind, pl.ds(0, count, 2), :] = values[kind]
            spread[slot, kind, pl.ds(1, count, 2), :] = values[kind]
        return tuple(spread[slot, kind, 0 : 2 * count, :] for kind in range(3))

    def split(values, n):
        return tuple(part[n * BOX : (n + 1) * BOX, :] for part in values)

    level2 = []
    for n, boxes in enumerate(((0, 4, 5), (1, 5, 0))):
        biases = [left_bias if b < 2 else right_bias for b in boxes]
        level2.append(raised(level(q2[n * BOX : (n + 1) * BOX, :], kv2, boxes, biases), 2))

    for message in (a_in, b_in, c_in):
        arrive(message)
    level3 = raised(level(q3, kv3, (0, 1, 2), [bias(has_a), bias(has_b), bias(has_c)]), 3)
    for message in d_in + e_in:
        arrive(message)
    level4 = raised(level(q4, kv4, (0, 1), [None, bias(has_e)]), 4)

    coarse = merge(level3, doubled(level4, 0))
    coarse = doubled(coarse, 1)
    for n in range(2):
        two = doubled(merge(level2[n], split(coarse, n)), 2 + n)
        for m in range(2):
            one = doubled(merge(kept(terms1, 2 * n + m), split(two, m)), 4 + 2 * n + m)
            for i in range(2):
                b = 4 * n + 2 * m + i
                _, total, numerator = merge(kept(terms0, b), split(one, i))
                done[b * BOX : (b + 1) * BOX, :] = (numerator / total).astype(jnp.bfloat16)

    back = [
        send(done.at[head(lax.rem(rank + step, ROWS)), :], out_ref.at[:, head(rank)], ring(step))
        for step in range(1, ROWS)
    ]
    own_out = pltpu.make_async_copy(done.at[head(rank), :], out_ref.at[:, head(rank)], load_sem.at[5])
    own_out.start()
    own_out.wait()
    for message in back:
        arrive(message)
    for copy, present in sent:
        when(present, copy.wait_send)


MESSAGES = 3 * (ROWS - 1) + 13


def solution(mesh):
    zs = mesh.shape["ctx"] // ROWS

    def step(q, k, v):
        anywhere = pl.BlockSpec(memory_space=pl.ANY)
        return pl.pallas_call(
            functools.partial(kernel, zs),
            out_shape=jax.ShapeDtypeStruct(q.shape, jnp.bfloat16),
            in_specs=[anywhere] * 3,
            out_specs=pl.BlockSpec(memory_space=pltpu.VMEM),
            scratch_shapes=[
                pltpu.VMEM((3, BOX, HEADS * BOX), jnp.bfloat16),
                pltpu.VMEM((8 * BOX, BOX), jnp.bfloat16),
                pltpu.VMEM((4 * BOX, BOX), jnp.bfloat16),
                pltpu.VMEM((2 * BOX, BOX), jnp.bfloat16),
                pltpu.VMEM((2, 10 * BOX, BOX), jnp.bfloat16),
                pltpu.VMEM((2, 8 * BOX, BOX), jnp.bfloat16),
                pltpu.VMEM((2, 6 * BOX, BOX), jnp.bfloat16),
                pltpu.VMEM((2, 4 * BOX, BOX), jnp.bfloat16),
                pltpu.VMEM((2, 5 * BOX // 2, BOX), jnp.bfloat16),
                pltpu.VMEM((3, 8 * BOX, BOX), jnp.float32),
                pltpu.VMEM((3, 4 * BOX, BOX), jnp.float32),
                pltpu.VMEM((8, 3, 2 * BOX, BOX), jnp.float32),
                pltpu.VMEM((8 * BOX, BOX), jnp.bfloat16),
                pltpu.SemaphoreType.DMA((6,)),
                pltpu.SemaphoreType.DMA((MESSAGES,)),
                pltpu.SemaphoreType.DMA((MESSAGES,)),
            ],
            compiler_params=pltpu.CompilerParams(
                collective_id=0, has_side_effects=True, vmem_limit_bytes=60 * 2**20
            ),
            cost_estimate=pl.CostEstimate(flops=400_000_000, bytes_accessed=2**20, transcendentals=800_000),
            name="attention",
        )(q, k, v)

    spec = P(("doc", "ctx"), None)
    return jax.shard_map(step, mesh=mesh, in_specs=(spec,) * 3, out_specs=spec, check_vma=False)
```

time: 242 us -> 42.1 us (0.17)
  the two profiles are of different devices: /device:TPU:252 before, /device:TPU:1 now
where the time goes in v1:
time: 42.1 us; the launch traced here: 42 us
  Pallas kernels  40.3 us (96%)
  local copies, waits for them, and re-layouts  1.67 us (4%)
    pallas_call x1, Pallas kernels, step(): pl.pallas_call(functools.partial(kernel, zs), out_shape=jax.ShapeDtypeStr...  40.3 us
    unnamed x1, local copies, waits for them, and re-layouts  1.67 us

profile of v1, /device:TPU:1, one launch (start us, length us, event | category | flops | bytes accessed | tf_op | source)
XLA Modules:
  0.0 42.0 jit_solution(3679851593742604671)
XLA Ops:
  0.0 40.3 %attention.1 = bf16[128,1024]{1,0:T(8,128)(2,1)} custom-call(bf16[128,1024]{1,0:T(8,128)(2,1)} %q_hbm.1, bf16[128,1024]{1,0:T(8,128)(2,1)} %k_hbm.1, bf16[128,1024]{1,0:T(8,128)(2,1)} %v_hbm.1), custom_call_target="tpu_custom_call" | custom-call | flops 400000000 | bytes 1048576 | tf_op jit(solution)/shard_map/attention/pallas_call | solution.py:296
  40.3 1.7 %copy.5 = bf16[128,1024]{1,0:T(8,128)(2,1)} copy(bf16[128,1024]{1,0:T(8,128)(2,1)} %attention.1) | data formatting | bytes 524288

commit v2 on v1

v2 whole, which is shorter than its diff:
```python
import functools
import math

import jax
import jax.numpy as jnp
from jax import lax
from jax.experimental import pallas as pl
from jax.experimental.pallas import tpu as pltpu
from jax.sharding import PartitionSpec as P

MESH = pl.DeviceIdType.MESH
HEADS = 8
BOX = 128
ROWS = 8
MASKED = -1e30
TO_LOG2 = math.log2(math.e) / math.sqrt(128.0)


def pool(rows):
    count = rows.shape[0]
    target = lax.broadcasted_iota(jnp.int32, (count // 2, count), 0)
    source = lax.broadcasted_iota(jnp.int32, (count // 2, count), 1)
    pairs = jnp.where(source // 2 == target, 0.5, 0.0).astype(jnp.bfloat16)
    return jnp.dot(pairs, rows, preferred_element_type=jnp.float32).astype(jnp.bfloat16)


def attend(query, keys, values, biases):
    scores = []
    for key, bias in zip(keys, biases):
        score = lax.dot_general(query, key, (((1,), (1,)), ((), ())), preferred_element_type=jnp.float32) * TO_LOG2
        scores.append(score if bias is None else score + bias)
    peak = jnp.max(functools.reduce(jnp.maximum, scores), axis=1, keepdims=True)
    shifted = [jnp.exp2(score - peak) for score in scores]
    total = jnp.sum(functools.reduce(jnp.add, shifted), axis=1, keepdims=True)
    weights = jnp.concatenate([part.astype(jnp.bfloat16) for part in shifted], axis=1)
    numerator = jnp.dot(weights, jnp.concatenate(values, axis=0), preferred_element_type=jnp.float32)
    return jnp.broadcast_to(peak, numerator.shape), jnp.broadcast_to(total, numerator.shape), numerator


def merge(one, other):
    newest = jnp.maximum(one[0], other[0])
    keep_one = jnp.exp2(one[0] - newest)
    keep_other = jnp.exp2(other[0] - newest)
    return newest, one[1] * keep_one + other[1] * keep_other, one[2] * keep_one + other[2] * keep_other


def kernel(zs, q_hbm, k_hbm, v_hbm, out_ref, source, far, q0, q1, q2, kv0, kv1, kv2, kv3, kv4, terms, ups, done, load_sem, send_sem, recv_sem, round_sem):
    me = lax.axis_index("ctx")
    z = me // ROWS
    rank = lax.rem(me, ROWS)
    y, core = rank // 2, lax.rem(rank, 2)
    odd = lax.rem(z, 2)

    def ring(turn, flip):
        return 2 * lax.rem(y + turn, 4) + lax.rem(core + flip, 2)

    def column(other):
        return lax.rem(other + zs, zs) * ROWS + rank

    def mate(other):
        return other + 1 - 2 * lax.rem(other, 2)

    peers = [(2, 0), (2, 1), (1, 0), (1, 1), (3, 0), (3, 1), (0, 1)]
    opposite = lax.rem(z + zs // 2, zs)
    mirrored = zs - 1 - z
    has_left = z > 0
    has_right = z < zs - 1
    has_a = z >= 2
    has_b = z < zs - 2
    has_c = ((odd == 0) & (z + 3 < zs)) | ((odd == 1) & (z >= 3))
    has_e = (z < 2) | (z >= zs - 2)

    loads = [
        pltpu.make_async_copy(ref, source.at[n], load_sem.at[n]) for n, ref in enumerate((k_hbm, v_hbm, q_hbm))
    ]
    for load in loads:
        load.start()

    def when(present, action):
        if present is None:
            action()
        else:
            pl.when(present)(action)

    def signal(semaphore, device):
        pl.semaphore_signal(semaphore, inc=1, device_id={"ctx": device}, device_id_type=MESH)

    barrier = pltpu.get_barrier_semaphore()
    for turn, flip in peers:
        signal(barrier, z * ROWS + ring(turn, flip))
    when(has_left, lambda: signal(barrier, column(z - 1)))
    when(has_right, lambda: signal(barrier, column(z + 1)))

    def blank(ref, present, start, count):
        @pl.when(jnp.logical_not(present))
        def _():
            ref[:, start : start + count, :] = jnp.zeros((2, count, BOX), jnp.bfloat16)

    blank(kv0, has_left, 0, BOX)
    blank(kv0, has_right, 9 * BOX, BOX)
    blank(kv1, has_left, 0, 2 * BOX)
    blank(kv1, has_right, 6 * BOX, 2 * BOX)
    blank(kv2, has_left, 0, BOX)
    blank(kv2, has_right, 5 * BOX, BOX)
    blank(kv3, has_a, 0, BOX)
    blank(kv3, has_b, BOX, BOX)
    blank(kv3, has_c, 2 * BOX, BOX)
    blank(kv4, has_e, BOX, BOX)

    used = [0]
    sent = []

    def remote(src, dst, device):
        number = used[0]
        used[0] += 1
        return pltpu.make_async_remote_copy(
            src_ref=src,
            dst_ref=dst,
            send_sem=send_sem.at[number],
            recv_sem=recv_sem.at[number],
            device_id={"ctx": device},
            device_id_type=MESH,
        )

    def send(src, dst, device, goes=None, comes=None):
        copy = remote(src, dst, device)
        when(goes, copy.start)
        sent.append((copy, goes))
        return copy, comes

    def arrive(message):
        when(message[1], message[0].wait_recv)

    def head(number):
        return pl.ds(pl.multiple_of(number * BOX, BOX), BOX)

    third = BOX // 8
    for kind in range(2):
        loads[kind].wait()
        far[kind] = pool(pool(pool(source[kind])))
    pl.semaphore_wait(barrier, ROWS - 1 + (z + zs - 1) // zs + (2 * zs - 2 - z) // zs)

    own_third = pl.ds(pl.multiple_of(3 * BOX + rank * third, third), third)
    far_in = [
        send(far.at[:, :, head(ring(turn, flip))], kv3.at[:, own_third, :], z * ROWS + ring(turn, flip))
        for turn, flip in peers
    ]
    kv_in = {
        (turn, flip): send(
            source.at[pl.ds(0, 2), :, head(ring(turn, flip))], kv0.at[:, head(rank + 1), :], z * ROWS + ring(turn, flip)
        )
        for turn, flip in peers
    }
    own_kv = pltpu.make_async_copy(source.at[pl.ds(0, 2), :, head(rank)], kv0.at[:, head(rank + 1), :], load_sem.at[3])
    own_kv.start()
    loads[2].wait()
    q_in = [
        send(source.at[2, :, head(ring(turn, flip))], q0.at[head(rank), :], z * ROWS + ring(turn, flip))
        for turn, flip in peers
    ]
    own_q = pltpu.make_async_copy(source.at[2, :, head(rank)], q0.at[head(rank), :], load_sem.at[4])
    own_q.start()
    kv3[:, own_third, :] = far[:, :, head(rank)]

    for turn in range(3):
        reach = 1 << turn
        below, above = z >= reach, z < zs - reach
        when(below, lambda: signal(round_sem.at[turn], column(z - reach)))
        when(above, lambda: signal(round_sem.at[turn], column(z + reach)))
        pl.semaphore_wait(round_sem.at[turn], (z + zs - reach) // zs + (2 * zs - 1 - z - reach) // zs)

    for message in far_in:
        arrive(message)
    for kind in range(2):
        kv4[kind, 2 * BOX : 2 * BOX + BOX // 2, :] = pool(kv3[kind, 3 * BOX : 4 * BOX, :])
    own4 = kv4.at[:, pl.ds(2 * BOX, BOX // 2), :]
    half = pl.multiple_of(odd * (BOX // 2), BOX // 2)
    far4_in = [
        send(own4, kv4.at[:, pl.ds(BOX + half, BOX // 2), :], column(mate(mirrored)), has_e, has_e),
        send(own4, kv4.at[:, pl.ds(BOX + half, BOX // 2), :], column(mirrored), has_e, has_e),
        send(own4, kv4.at[:, pl.ds(half, BOX // 2), :], column(opposite)),
        send(own4, kv4.at[:, pl.ds(half, BOX // 2), :], column(mate(opposite))),
    ]
    own3 = kv3.at[:, pl.ds(3 * BOX, BOX), :]
    a_in = send(own3, kv3.at[:, pl.ds(0, BOX), :], column(z + 2), has_b, has_a)
    b_in = send(own3, kv3.at[:, pl.ds(BOX, BOX), :], column(z - 2), has_a, has_b)

    left0 = remote(kv0.at[:, pl.ds(8 * BOX, BOX), :], kv0.at[:, pl.ds(0, BOX), :], column(z + 1))
    right0 = remote(kv0.at[:, pl.ds(BOX, BOX), :], kv0.at[:, pl.ds(9 * BOX, BOX), :], column(z - 1))
    own_kv.wait()
    near1 = []
    for turn in (0, 1, 3, 2):
        chip = lax.rem(y + turn, 4)
        back = (4 - turn) % 4
        for flip in range(2):
            if (back, flip) in kv_in:
                arrive(kv_in[back, flip])
        when((chip == 3) & has_right, left0.start)
        when((chip == 0) & has_left, right0.start)
        pair = pl.ds(pl.multiple_of((2 * chip + 1) * BOX, BOX), 2 * BOX)
        for kind in range(2):
            kv1[kind, head(2 + chip), :] = pool(kv0[kind, pair, :])
        up = chip >= 2
        near1.append(
            send(
                kv1.at[:, head(2 + chip), :],
                kv1.at[:, head(lax.rem(chip + 6, 8)), :],
                column(z - 1 + 2 * (chip // 2)),
                (up & has_right) | (jnp.logical_not(up) & has_left),
                (up & has_left) | (jnp.logical_not(up) & has_right),
            )
        )
    for kind in range(2):
        for n in range(2):
            kv2[kind, (2 + n) * BOX : (3 + n) * BOX, :] = pool(kv1[kind, (2 * n + 2) * BOX : (2 * n + 4) * BOX, :])
    left2 = send(kv2.at[:, pl.ds(2 * BOX, BOX), :], kv2.at[:, pl.ds(0, BOX), :], column(z + 1), has_right, has_left)
    right2 = send(kv2.at[:, pl.ds(3 * BOX, BOX), :], kv2.at[:, pl.ds(5 * BOX, BOX), :], column(z - 1), has_left, has_right)

    arrive(a_in)
    arrive(b_in)
    c_in = send(
        kv3.at[:, head(odd), :],
        kv3.at[:, pl.ds(2 * BOX, BOX), :],
        column(mate(z)),
        ((odd == 0) & has_a) | ((odd == 1) & has_b),
        has_c,
    )

    def bias(present):
        return jnp.where(present, 0.0, MASKED).astype(jnp.float32)

    left_bias, right_bias = bias(has_left), bias(has_right)

    own_q.wait()
    for message in q_in:
        arrive(message)
    for n in range(4):
        q1[n * BOX : (n + 1) * BOX, :] = pool(q0[2 * n * BOX : (2 * n + 2) * BOX, :])
    for n in range(2):
        q2[n * BOX : (n + 1) * BOX, :] = pool(q1[2 * n * BOX : (2 * n + 2) * BOX, :])
    q3 = pool(q2[...])
    q4 = pool(q3)

    def box(ref, kind, start):
        return ref[kind, start * BOX : (start + 1) * BOX, :]

    def level(query, ref, boxes, biases):
        return attend(query, [box(ref, 0, b) for b in boxes], [box(ref, 1, b) for b in boxes], biases)

    def keep(n, values):
        for kind in range(3):
            terms[kind, n * BOX : (n + 1) * BOX, :] = values[kind]

    def kept(n):
        return tuple(terms[kind, n * BOX : (n + 1) * BOX, :] for kind in range(3))

    def level0(n):
        biases = [left_bias if n == 0 else None, None, right_bias if n == ROWS - 1 else None]
        keep(n, level(q0[n * BOX : (n + 1) * BOX, :], kv0, (n, n + 1, n + 2), biases))

    def raised(values, height):
        return values[0] + float(height), values[1], values[2]

    def repeated(values, start, times):
        count = values[0].shape[0]
        for kind in range(3):
            for turn in range(times):
                ups[kind, pl.ds(start + turn, count, times), :] = values[kind]

    def risen(start, count):
        return tuple(ups[kind, start : start + count, :] for kind in range(3))

    for n in range(1, ROWS - 1):
        level0(n)
    for message in near1:
        arrive(message)
    for kind in range(2):
        kv2[kind, BOX : 2 * BOX, :] = pool(kv1[kind, 0 : 2 * BOX, :])
        kv2[kind, 4 * BOX : 5 * BOX, :] = pool(kv1[kind, 6 * BOX : 8 * BOX, :])
    level1 = []
    for n, boxes in enumerate(((0, 4, 5), (1, 5, 0), (2, 6, 7), (3, 7, 2))):
        biases = [left_bias if b < 2 else right_bias if b >= 6 else None for b in boxes]
        level1.append(raised(level(q1[n * BOX : (n + 1) * BOX, :], kv1, boxes, biases), 1))
    when(has_left, left0.wait_recv)
    when(has_right, right0.wait_recv)
    level0(0)
    level0(ROWS - 1)
    arrive(left2)
    arrive(right2)
    for n, boxes in enumerate(((0, 4, 5), (1, 5, 0))):
        biases = [left_bias if b < 2 else right_bias for b in boxes]
        level2 = raised(level(q2[n * BOX : (n + 1) * BOX, :], kv2, boxes, biases), 2)
        repeated(level2, 2 * n * BOX, 2)
        for m in range(2):
            repeated(merge(level1[2 * n + m], risen((2 * n + m) * BOX, BOX)), 8 * BOX + 2 * (2 * n + m) * BOX, 2)
    for n in range(ROWS):
        keep(n, merge(kept(n), risen((8 + n) * BOX, BOX)))

    arrive(c_in)
    level3 = raised(level(q3, kv3, (0, 1, 2), [bias(has_a), bias(has_b), bias(has_c)]), 3)
    for message in far4_in:
        arrive(message)
    repeated(raised(level(q4, kv4, (0, 1), [None, bias(has_e)]), 4), 0, 2)
    repeated(merge(level3, risen(0, BOX)), 8 * BOX, 8)

    def finish(number):
        fine = tuple(terms[kind, head(number), :] for kind in range(3))
        coarse = tuple(ups[kind, head(8 + number), :] for kind in range(3))
        _, total, numerator = merge(fine, coarse)
        done[head(number), :] = (numerator / total).astype(jnp.bfloat16)

    home = []
    for turn, flip in peers:
        number = ring(turn, flip)
        finish(number)
        home.append(send(done.at[head(number), :], out_ref.at[:, head(rank)], z * ROWS + number))
    finish(rank)
    own_out = pltpu.make_async_copy(done.at[head(rank), :], out_ref.at[:, head(rank)], load_sem.at[5])
    own_out.start()
    own_out.wait()
    for message in home:
        arrive(message)
    for copy, goes in sent:
        when(goes, copy.wait_send)
    when(has_right, left0.wait_send)
    when(has_left, right0.wait_send)


MESSAGES = 4 * (ROWS - 1) + 15


def solution(mesh):
    zs = mesh.shape["ctx"] // ROWS

    def step(q, k, v):
        anywhere = pl.BlockSpec(memory_space=pl.ANY)
        return pl.pallas_call(
            functools.partial(kernel, zs),
            out_shape=jax.ShapeDtypeStruct(q.shape, jnp.bfloat16),
            in_specs=[anywhere] * 3,
            out_specs=pl.BlockSpec(memory_space=pltpu.VMEM),
            scratch_shapes=[
                pltpu.VMEM((3, BOX, HEADS * BOX), jnp.bfloat16),
                pltpu.VMEM((2, BOX // 8, HEADS * BOX), jnp.bfloat16),
                pltpu.VMEM((8 * BOX, BOX), jnp.bfloat16),
                pltpu.VMEM((4 * BOX, BOX), jnp.bfloat16),
                pltpu.VMEM((2 * BOX, BOX), jnp.bfloat16),
                pltpu.VMEM((2, 10 * BOX, BOX), jnp.bfloat16),
                pltpu.VMEM((2, 8 * BOX, BOX), jnp.bfloat16),
                pltpu.VMEM((2, 6 * BOX, BOX), jnp.bfloat16),
                pltpu.VMEM((2, 4 * BOX, BOX), jnp.bfloat16),
                pltpu.VMEM((2, 5 * BOX // 2, BOX), jnp.bfloat16),
                pltpu.VMEM((3, 8 * BOX, BOX), jnp.float32),
                pltpu.VMEM((3, 16 * BOX, BOX), jnp.float32),
                pltpu.VMEM((8 * BOX, BOX), jnp.bfloat16),
                pltpu.SemaphoreType.DMA((6,)),
                pltpu.SemaphoreType.DMA((MESSAGES,)),
                pltpu.SemaphoreType.DMA((MESSAGES,)),
                pltpu.SemaphoreType.REGULAR((3,)),
            ],
            compiler_params=pltpu.CompilerParams(
                collective_id=0, has_side_effects=True, vmem_limit_bytes=60 * 2**20
            ),
            cost_estimate=pl.CostEstimate(flops=400_000_000, bytes_accessed=2**20, transcendentals=800_000),
            name="attention",
        )(q, k, v)

    spec = P(("doc", "ctx"), None)
    return jax.shard_map(step, mesh=mesh, in_specs=(spec,) * 3, out_specs=spec, check_vma=False)
```

time: 42.1 us -> 37.6 us (0.89)
  Pallas kernels: 40.3 us -> 35.8 us
    pallas_call x1, Pallas kernels: 40.3 us -> 35.8 us  [step(): pl.pallas_call(functools.partial(kernel, zs), out_shape=jax.ShapeDtypeStr...]
where the time goes in v2:
time: 37.6 us; the launch traced here: 37.5 us
  Pallas kernels  35.8 us (95%)
  local copies, waits for them, and re-layouts  1.67 us (4%)
    pallas_call x1, Pallas kernels, step(): pl.pallas_call(functools.partial(kernel, zs), out_shape=jax.ShapeDtypeStr...  35.8 us
    unnamed x1, local copies, waits for them, and re-layouts  1.67 us

profile of v2, /device:TPU:1, one launch (start us, length us, event | category | flops | bytes accessed | tf_op | source)
XLA Modules:
  0.0 37.5 jit_solution(7803269733434544494)
XLA Ops:
  0.0 35.8 %attention.1 = bf16[128,1024]{1,0:T(8,128)(2,1)} custom-call(bf16[128,1024]{1,0:T(8,128)(2,1)} %q_hbm.1, bf16[128,1024]{1,0:T(8,128)(2,1)} %k_hbm.1, bf16[128,1024]{1,0:T(8,128)(2,1)} %v_hbm.1), custom_call_target="tpu_custom_call" | custom-call | flops 400000000 | bytes 1048576 | tf_op jit(solution)/shard_map/attention/pallas_call | solution.py:337
  35.8 1.7 %copy.5 = bf16[128,1024]{1,0:T(8,128)(2,1)} copy(bf16[128,1024]{1,0:T(8,128)(2,1)} %attention.1) | data formatting | bytes 524288

commit v3 on v2

--- a/solution.py
+++ b/solution.py
@@ -44,7 +44,7 @@
     return newest, one[1] * keep_one + other[1] * keep_other, one[2] * keep_one + other[2] * keep_other
 
 
-def kernel(zs, q_hbm, k_hbm, v_hbm, out_ref, source, far, q0, q1, q2, kv0, kv1, kv2, kv3, kv4, terms, ups, done, load_sem, send_sem, recv_sem, round_sem):
+def kernel(zs, q_hbm, k_hbm, v_hbm, out_hbm, source, half1, far, near, relay, q1, q2, kv1, kv2, kv3, kv4, terms, ups, parcel, inbox, done, load_sem, send_sem, recv_sem, round_sem):
     me = lax.axis_index("ctx")
     z = me // ROWS
     rank = lax.rem(me, ROWS)
@@ -96,8 +96,6 @@
         def _():
             ref[:, start : start + count, :] = jnp.zeros((2, count, BOX), jnp.bfloat16)
 
-    blank(kv0, has_left, 0, BOX)
-    blank(kv0, has_right, 9 * BOX, BOX)
     blank(kv1, has_left, 0, 2 * BOX)
     blank(kv1, has_right, 6 * BOX, 2 * BOX)
     blank(kv2, has_left, 0, BOX)
@@ -106,6 +104,17 @@
     blank(kv3, has_b, BOX, BOX)
     blank(kv3, has_c, 2 * BOX, BOX)
     blank(kv4, has_e, BOX, BOX)
+
+    starts = (z == 0) & (rank == 0)
+    ends = (z == zs - 1) & (rank == ROWS - 1)
+
+    @pl.when(starts)
+    def _():
+        near[0] = jnp.zeros(near.shape[1:], jnp.bfloat16)
+
+    @pl.when(ends)
+    def _():
+        near[1] = jnp.zeros(near.shape[1:], jnp.bfloat16)
 
     used = [0]
     sent = []
@@ -137,57 +146,76 @@
     third = BOX // 8
     for kind in range(2):
         loads[kind].wait()
-        far[kind] = pool(pool(pool(source[kind])))
+        half1[kind] = pool(source[kind])
+        far[kind] = pool(pool(half1[kind]))
     pl.semaphore_wait(barrier, ROWS - 1 + (z + zs - 1) // zs + (2 * zs - 2 - z) // zs)
 
     own_third = pl.ds(pl.multiple_of(3 * BOX + rank * third, third), third)
+    own_half = pl.ds(pl.multiple_of(2 * BOX + rank * (BOX // 2), BOX // 2), BOX // 2)
+    own_query = pl.ds(pl.multiple_of(rank * (BOX // 2), BOX // 2), BOX // 2)
     far_in = [
         send(far.at[:, :, head(ring(turn, flip))], kv3.at[:, own_third, :], z * ROWS + ring(turn, flip))
         for turn, flip in peers
     ]
     kv_in = {
         (turn, flip): send(
-            source.at[pl.ds(0, 2), :, head(ring(turn, flip))], kv0.at[:, head(rank + 1), :], z * ROWS + ring(turn, flip)
+            half1.at[pl.ds(0, 2), :, head(ring(turn, flip))], kv1.at[:, own_half, :], z * ROWS + ring(turn, flip)
         )
         for turn, flip in peers
     }
-    own_kv = pltpu.make_async_copy(source.at[pl.ds(0, 2), :, head(rank)], kv0.at[:, head(rank + 1), :], load_sem.at[3])
-    own_kv.start()
     loads[2].wait()
+    half1[2] = pool(source[2])
     q_in = [
-        send(source.at[2, :, head(ring(turn, flip))], q0.at[head(rank), :], z * ROWS + ring(turn, flip))
+        send(half1.at[2, :, head(ring(turn, flip))], q1.at[own_query, :], z * ROWS + ring(turn, flip))
         for turn, flip in peers
     ]
-    own_q = pltpu.make_async_copy(source.at[2, :, head(rank)], q0.at[head(rank), :], load_sem.at[4])
-    own_q.start()
+    last = rank // (ROWS - 1)
+    at_end = (rank == 0) | (rank == ROWS - 1)
+    towards = (last == 1) & has_right | (rank == 0) & has_left
+    behind = (last == 1) & has_left | (rank == 0) & has_right
+    relay_in = send(source.at[pl.ds(0, 2)], relay, column(z - 1 + 2 * last), towards, behind)
+
     kv3[:, own_third, :] = far[:, :, head(rank)]
-
-    for turn in range(3):
+    kv1[:, own_half, :] = half1[0:2, :, head(rank)]
+    q1[own_query, :] = half1[2, :, head(rank)]
+
+    def tell(turn):
         reach = 1 << turn
-        below, above = z >= reach, z < zs - reach
-        when(below, lambda: signal(round_sem.at[turn], column(z - reach)))
-        when(above, lambda: signal(round_sem.at[turn], column(z + reach)))
+        when(z >= reach, lambda: signal(round_sem.at[turn], column(z - reach)))
+        when(z < zs - reach, lambda: signal(round_sem.at[turn], column(z + reach)))
+
+    def hear(turn):
+        reach = 1 << turn
         pl.semaphore_wait(round_sem.at[turn], (z + zs - reach) // zs + (2 * zs - 1 - z - reach) // zs)
 
+    tell(0)
+    hear(0)
+    tell(1)
     for message in far_in:
         arrive(message)
-    for kind in range(2):
-        kv4[kind, 2 * BOX : 2 * BOX + BOX // 2, :] = pool(kv3[kind, 3 * BOX : 4 * BOX, :])
-    own4 = kv4.at[:, pl.ds(2 * BOX, BOX // 2), :]
-    half = pl.multiple_of(odd * (BOX // 2), BOX // 2)
-    far4_in = [
-        send(own4, kv4.at[:, pl.ds(BOX + half, BOX // 2), :], column(mate(mirrored)), has_e, has_e),
-        send(own4, kv4.at[:, pl.ds(BOX + half, BOX // 2), :], column(mirrored), has_e, has_e),
-        send(own4, kv4.at[:, pl.ds(half, BOX // 2), :], column(opposite)),
-        send(own4, kv4.at[:, pl.ds(half, BOX // 2), :], column(mate(opposite))),
-    ]
     own3 = kv3.at[:, pl.ds(3 * BOX, BOX), :]
     a_in = send(own3, kv3.at[:, pl.ds(0, BOX), :], column(z + 2), has_b, has_a)
     b_in = send(own3, kv3.at[:, pl.ds(BOX, BOX), :], column(z - 2), has_a, has_b)
-
-    left0 = remote(kv0.at[:, pl.ds(8 * BOX, BOX), :], kv0.at[:, pl.ds(0, BOX), :], column(z + 1))
-    right0 = remote(kv0.at[:, pl.ds(BOX, BOX), :], kv0.at[:, pl.ds(9 * BOX, BOX), :], column(z - 1))
-    own_kv.wait()
+    for kind in range(2):
+        kv4[kind, 2 * BOX : 2 * BOX + BOX // 2, :] = pool(kv3[kind, 3 * BOX : 4 * BOX, :])
+    hear(1)
+    tell(2)
+    own4 = kv4.at[:, pl.ds(2 * BOX, BOX // 2), :]
+    half = pl.multiple_of(odd * (BOX // 2), BOX // 2)
+    far4 = [
+        (remote(own4, kv4.at[:, pl.ds(BOX + half, BOX // 2), :], column(mate(mirrored))), has_e),
+        (remote(own4, kv4.at[:, pl.ds(BOX + half, BOX // 2), :], column(mirrored)), has_e),
+        (remote(own4, kv4.at[:, pl.ds(half, BOX // 2), :], column(opposite)), z >= 0),
+        (remote(own4, kv4.at[:, pl.ds(half, BOX // 2), :], column(mate(opposite))), z >= 0),
+    ]
+    sent.extend(far4)
+
+    def send_far4(chosen):
+        when(chosen, lambda: hear(2))
+        for copy, goes in far4:
+            when(chosen & goes, copy.start)
+
+    send_far4(z >= zs // 2)
     near1 = []
     for turn in (0, 1, 3, 2):
         chip = lax.rem(y + turn, 4)
@@ -195,11 +223,6 @@
         for flip in range(2):
             if (back, flip) in kv_in:
                 arrive(kv_in[back, flip])
-        when((chip == 3) & has_right, left0.start)
-        when((chip == 0) & has_left, right0.start)
-        pair = pl.ds(pl.multiple_of((2 * chip + 1) * BOX, BOX), 2 * BOX)
-        for kind in range(2):
-            kv1[kind, head(2 + chip), :] = pool(kv0[kind, pair, :])
         up = chip >= 2
         near1.append(
             send(
@@ -216,6 +239,13 @@
     left2 = send(kv2.at[:, pl.ds(2 * BOX, BOX), :], kv2.at[:, pl.ds(0, BOX), :], column(z + 1), has_right, has_left)
     right2 = send(kv2.at[:, pl.ds(3 * BOX, BOX), :], kv2.at[:, pl.ds(5 * BOX, BOX), :], column(z - 1), has_left, has_right)
 
+    send_far4(z < zs // 2)
+
+    right0 = send(source.at[pl.ds(0, 2)], near.at[0], me + 1, rank < ROWS - 1, rank > 0)
+    left0 = send(source.at[pl.ds(0, 2)], near.at[1], me - 1, rank > 0, rank < ROWS - 1)
+    arrive(relay_in)
+    around0 = send(relay, near.at[1 - last], z * ROWS + ROWS - 1 - rank, behind, towards)
+
     arrive(a_in)
     arrive(b_in)
     c_in = send(
@@ -231,11 +261,8 @@
 
     left_bias, right_bias = bias(has_left), bias(has_right)
 
-    own_q.wait()
     for message in q_in:
         arrive(message)
-    for n in range(4):
-        q1[n * BOX : (n + 1) * BOX, :] = pool(q0[2 * n * BOX : (2 * n + 2) * BOX, :])
     for n in range(2):
         q2[n * BOX : (n + 1) * BOX, :] = pool(q1[2 * n * BOX : (2 * n + 2) * BOX, :])
     q3 = pool(q2[...])
@@ -246,17 +273,6 @@
 
     def level(query, ref, boxes, biases):
         return attend(query, [box(ref, 0, b) for b in boxes], [box(ref, 1, b) for b in boxes], biases)
-
-    def keep(n, values):
-        for kind in range(3):
-            terms[kind, n * BOX : (n + 1) * BOX, :] = values[kind]
-
-    def kept(n):
-        return tuple(terms[kind, n * BOX : (n + 1) * BOX, :] for kind in range(3))
-
-    def level0(n):
-        biases = [left_bias if n == 0 else None, None, right_bias if n == ROWS - 1 else None]
-        keep(n, level(q0[n * BOX : (n + 1) * BOX, :], kv0, (n, n + 1, n + 2), biases))
 
     def raised(values, height):
         return values[0] + float(height), values[1], values[2]
@@ -270,8 +286,6 @@
     def risen(start, count):
         return tuple(ups[kind, start : start + count, :] for kind in range(3))
 
-    for n in range(1, ROWS - 1):
-        level0(n)
     for message in near1:
         arrive(message)
     for kind in range(2):
@@ -281,10 +295,6 @@
     for n, boxes in enumerate(((0, 4, 5), (1, 5, 0), (2, 6, 7), (3, 7, 2))):
         biases = [left_bias if b < 2 else right_bias if b >= 6 else None for b in boxes]
         level1.append(raised(level(q1[n * BOX : (n + 1) * BOX, :], kv1, boxes, biases), 1))
-    when(has_left, left0.wait_recv)
-    when(has_right, right0.wait_recv)
-    level0(0)
-    level0(ROWS - 1)
     arrive(left2)
     arrive(right2)
     for n, boxes in enumerate(((0, 4, 5), (1, 5, 0))):
@@ -292,41 +302,80 @@
         level2 = raised(level(q2[n * BOX : (n + 1) * BOX, :], kv2, boxes, biases), 2)
         repeated(level2, 2 * n * BOX, 2)
         for m in range(2):
-            repeated(merge(level1[2 * n + m], risen((2 * n + m) * BOX, BOX)), 8 * BOX + 2 * (2 * n + m) * BOX, 2)
-    for n in range(ROWS):
-        keep(n, merge(kept(n), risen((8 + n) * BOX, BOX)))
+            merged = merge(level1[2 * n + m], risen((2 * n + m) * BOX, BOX))
+            for kind in range(3):
+                terms[kind, (2 * n + m) * BOX : (2 * n + m + 1) * BOX, :] = merged[kind]
 
     arrive(c_in)
     level3 = raised(level(q3, kv3, (0, 1, 2), [bias(has_a), bias(has_b), bias(has_c)]), 3)
-    for message in far4_in:
+    for message in far4:
         arrive(message)
     repeated(raised(level(q4, kv4, (0, 1), [None, bias(has_e)]), 4), 0, 2)
-    repeated(merge(level3, risen(0, BOX)), 8 * BOX, 8)
-
-    def finish(number):
+    repeated(merge(level3, risen(0, BOX)), 4 * BOX, 4)
+
+    here = lax.broadcasted_iota(jnp.int32, (BOX // 2, BOX), 0) == lax.broadcasted_iota(jnp.int32, (BOX // 2, BOX), 1)
+    line = lax.broadcasted_iota(jnp.int32, (8, BOX), 0)
+
+    def finish(number, box_out):
+        rows = pl.ds(pl.multiple_of(number * (BOX // 2), BOX // 2), BOX // 2)
+        rows_up = pl.ds(pl.multiple_of(4 * BOX + number * (BOX // 2), BOX // 2), BOX // 2)
+        peak, total, numerator = merge(
+            tuple(terms[kind, rows, :] for kind in range(3)), tuple(ups[kind, rows_up, :] for kind in range(3))
+        )
+        peak_row, total_row = (
+            jnp.sum(jnp.where(here, part, 0.0), axis=0, keepdims=True) for part in (peak, total)
+        )
+        box_out[0 : BOX // 2, :] = numerator
+        box_out[BOX // 2 :, :] = jnp.where(line == 0, peak_row, jnp.where(line == 1, total_row, 0.0))
+
+    home = {}
+    for n, (turn, flip) in enumerate(peers):
+        finish(ring(turn, flip), parcel.at[n])
+        home[turn, flip] = send(parcel.at[n], inbox.at[rank], z * ROWS + ring(turn, flip))
+    finish(rank, inbox.at[rank])
+
+    arrive(right0)
+    arrive(left0)
+    arrive(around0)
+    start_bias, end_bias = bias(jnp.logical_not(starts)), bias(jnp.logical_not(ends))
+    for n in range(HEADS):
+        columns = slice(n * BOX, (n + 1) * BOX)
+        values = attend(
+            source[2, :, columns],
+            [near[0, 0, :, columns], source[0, :, columns], near[1, 0, :, columns]],
+            [near[0, 1, :, columns], source[1, :, columns], near[1, 1, :, columns]],
+            [start_bias, None, end_bias],
+        )
+        for kind in range(3):
+            terms[kind, n * BOX : (n + 1) * BOX, :] = values[kind]
+
+    out_copies = []
+    for n, (turn, flip) in enumerate([(0, 0)] + peers[::-1]):
+        if n:
+            arrive(home[turn, flip])
+        number = ring((4 - turn) % 4, flip)
+        got = inbox.at[number]
+        rows = got[BOX // 2 :, :]
+        coarse = [
+            jnp.broadcast_to(
+                jnp.sum(jnp.where(here, rows[row : row + 1, :], 0.0), axis=1, keepdims=True), (BOX // 2, BOX)
+            )
+            for row in range(2)
+        ]
+        repeated((coarse[0], coarse[1], got[0 : BOX // 2, :]), n * BOX, 2)
         fine = tuple(terms[kind, head(number), :] for kind in range(3))
-        coarse = tuple(ups[kind, head(8 + number), :] for kind in range(3))
-        _, total, numerator = merge(fine, coarse)
-        done[head(number), :] = (numerator / total).astype(jnp.bfloat16)
-
-    home = []
-    for turn, flip in peers:
-        number = ring(turn, flip)
-        finish(number)
-        home.append(send(done.at[head(number), :], out_ref.at[:, head(rank)], z * ROWS + number))
-    finish(rank)
-    own_out = pltpu.make_async_copy(done.at[head(rank), :], out_ref.at[:, head(rank)], load_sem.at[5])
-    own_out.start()
-    own_out.wait()
-    for message in home:
-        arrive(message)
+        _, total, numerator = merge(fine, risen(n * BOX, BOX))
+        done[:, head(number)] = (numerator / total).astype(jnp.bfloat16)
+        copy = pltpu.make_async_copy(done.at[:, head(number)], out_hbm.at[:, head(number)], load_sem.at[3 + n])
+        copy.start()
+        out_copies.append(copy)
     for copy, goes in sent:
         when(goes, copy.wait_send)
-    when(has_right, left0.wait_send)
-    when(has_left, right0.wait_send)
-
-
-MESSAGES = 4 * (ROWS - 1) + 15
+    for copy in out_copies:
+        copy.wait()
+
+
+MESSAGES = 4 * (ROWS - 1) + 17
 
 
 def solution(mesh):
@@ -338,22 +387,25 @@
             functools.partial(kernel, zs),
             out_shape=jax.ShapeDtypeStruct(q.shape, jnp.bfloat16),
             in_specs=[anywhere] * 3,
-            out_specs=pl.BlockSpec(memory_space=pltpu.VMEM),
+            out_specs=anywhere,
             scratch_shapes=[
                 pltpu.VMEM((3, BOX, HEADS * BOX), jnp.bfloat16),
+                pltpu.VMEM((3, BOX // 2, HEADS * BOX), jnp.bfloat16),
                 pltpu.VMEM((2, BOX // 8, HEADS * BOX), jnp.bfloat16),
-                pltpu.VMEM((8 * BOX, BOX), jnp.bfloat16),
+                pltpu.VMEM((2, 2, BOX, HEADS * BOX), jnp.bfloat16),
+                pltpu.VMEM((2, BOX, HEADS * BOX), jnp.bfloat16),
                 pltpu.VMEM((4 * BOX, BOX), jnp.bfloat16),
                 pltpu.VMEM((2 * BOX, BOX), jnp.bfloat16),
-                pltpu.VMEM((2, 10 * BOX, BOX), jnp.bfloat16),
                 pltpu.VMEM((2, 8 * BOX, BOX), jnp.bfloat16),
                 pltpu.VMEM((2, 6 * BOX, BOX), jnp.bfloat16),
                 pltpu.VMEM((2, 4 * BOX, BOX), jnp.bfloat16),
                 pltpu.VMEM((2, 5 * BOX // 2, BOX), jnp.bfloat16),
                 pltpu.VMEM((3, 8 * BOX, BOX), jnp.float32),
-                pltpu.VMEM((3, 16 * BOX, BOX), jnp.float32),
-                pltpu.VMEM((8 * BOX, BOX), jnp.bfloat16),
-                pltpu.SemaphoreType.DMA((6,)),
+                pltpu.VMEM((3, 8 * BOX, BOX), jnp.float32),
+                pltpu.VMEM((ROWS - 1, BOX // 2 + 8, BOX), jnp.float32),
+                pltpu.VMEM((ROWS, BOX // 2 + 8, BOX), jnp.float32),
+                pltpu.VMEM((BOX, HEADS * BOX), jnp.bfloat16),
+                pltpu.SemaphoreType.DMA((3 + HEADS,)),
                 pltpu.SemaphoreType.DMA((MESSAGES,)),
                 pltpu.SemaphoreType.DMA((MESSAGES,)),
                 pltpu.SemaphoreType.REGULAR((3,)),

time: 37.6 us -> 34.1 us (0.907)
  the two profiles are of different devices: /device:TPU:1 before, /device:TPU:121 now
where the time goes in v3:
time: 34.1 us; the launch traced here: 34 us
  Pallas kernels  32.3 us (95%)
  local copies, waits for them, and re-layouts  1.67 us (5%)
    pallas_call x1, Pallas kernels, step(): pl.pallas_call(functools.partial(kernel, zs), out_shape=jax.ShapeDtypeStr...  32.3 us
    unnamed x1, local copies, waits for them, and re-layouts  1.67 us

profile of v3, /device:TPU:121, one launch (start us, length us, event | category | flops | bytes accessed | tf_op | source)
XLA Modules:
  0.0 34.0 jit_solution(2983858078621212513)
XLA Ops:
  0.0 32.3 %attention.1 = bf16[128,1024]{1,0:T(8,128)(2,1)} custom-call(bf16[128,1024]{1,0:T(8,128)(2,1)} %q_hbm.1, bf16[128,1024]{1,0:T(8,128)(2,1)} %k_hbm.1, bf16[128,1024]{1,0:T(8,128)(2,1)} %v_hbm.1), custom_call_target="tpu_custom_call" | custom-call | flops 400000000 | bytes 1048576 | tf_op jit(solution)/shard_map/attention/pallas_call | solution.py:386
  32.3 1.7 %copy.5 = bf16[128,1024]{1,0:T(8,128)(2,1)} copy(bf16[128,1024]{1,0:T(8,128)(2,1)} %attention.1) | data formatting | bytes 524288

commit v4 on v3

--- a/solution.py
+++ b/solution.py
@@ -44,7 +44,7 @@
     return newest, one[1] * keep_one + other[1] * keep_other, one[2] * keep_one + other[2] * keep_other
 
 
-def kernel(zs, q_hbm, k_hbm, v_hbm, out_hbm, source, half1, far, near, relay, q1, q2, kv1, kv2, kv3, kv4, terms, ups, parcel, inbox, done, load_sem, send_sem, recv_sem, round_sem):
+def kernel(zs, q_hbm, k_hbm, v_hbm, out_ref, source, half1, far, near, relay, q1, q2, kv1, kv2, kv3, kv4, terms, ups, parcel, inbox, load_sem, send_sem, recv_sem, round_sem):
     me = lax.axis_index("ctx")
     z = me // ROWS
     rank = lax.rem(me, ROWS)
@@ -314,7 +314,7 @@
     repeated(merge(level3, risen(0, BOX)), 4 * BOX, 4)
 
     here = lax.broadcasted_iota(jnp.int32, (BOX // 2, BOX), 0) == lax.broadcasted_iota(jnp.int32, (BOX // 2, BOX), 1)
-    line = lax.broadcasted_iota(jnp.int32, (8, BOX), 0)
+    line = lax.broadcasted_iota(jnp.int32, (16, BOX), 0)
 
     def finish(number, box_out):
         rows = pl.ds(pl.multiple_of(number * (BOX // 2), BOX // 2), BOX // 2)
@@ -322,11 +322,12 @@
         peak, total, numerator = merge(
             tuple(terms[kind, rows, :] for kind in range(3)), tuple(ups[kind, rows_up, :] for kind in range(3))
         )
-        peak_row, total_row = (
-            jnp.sum(jnp.where(here, part, 0.0), axis=0, keepdims=True) for part in (peak, total)
-        )
-        box_out[0 : BOX // 2, :] = numerator
-        box_out[BOX // 2 :, :] = jnp.where(line == 0, peak_row, jnp.where(line == 1, total_row, 0.0))
+        box_out[0 : BOX // 2, :] = (numerator / total).astype(jnp.bfloat16)
+        weight = jnp.sum(jnp.where(here, peak + jnp.log2(total), 0.0), axis=0, keepdims=True)
+        high = weight.astype(jnp.bfloat16).astype(jnp.float32)
+        middle = (weight - high).astype(jnp.bfloat16).astype(jnp.float32)
+        parts = jnp.where(line == 0, high, jnp.where(line == 1, middle, weight - high - middle))
+        box_out[BOX // 2 :, :] = jnp.where(line < 3, parts, 0.0).astype(jnp.bfloat16)
 
     home = {}
     for n, (turn, flip) in enumerate(peers):
@@ -349,30 +350,21 @@
         for kind in range(3):
             terms[kind, n * BOX : (n + 1) * BOX, :] = values[kind]
 
-    out_copies = []
     for n, (turn, flip) in enumerate([(0, 0)] + peers[::-1]):
         if n:
             arrive(home[turn, flip])
         number = ring((4 - turn) % 4, flip)
         got = inbox.at[number]
-        rows = got[BOX // 2 :, :]
-        coarse = [
-            jnp.broadcast_to(
-                jnp.sum(jnp.where(here, rows[row : row + 1, :], 0.0), axis=1, keepdims=True), (BOX // 2, BOX)
-            )
-            for row in range(2)
-        ]
-        repeated((coarse[0], coarse[1], got[0 : BOX // 2, :]), n * BOX, 2)
+        parts = got[BOX // 2 :, :].astype(jnp.float32)
+        weight = parts[0:1, :] + parts[1:2, :] + parts[2:3, :]
+        weight = jnp.sum(jnp.where(here, weight, 0.0), axis=1, keepdims=True)
+        coarse = got[0 : BOX // 2, :].astype(jnp.float32)
+        repeated((jnp.broadcast_to(weight, coarse.shape), jnp.ones_like(coarse), coarse), n * BOX, 2)
         fine = tuple(terms[kind, head(number), :] for kind in range(3))
         _, total, numerator = merge(fine, risen(n * BOX, BOX))
-        done[:, head(number)] = (numerator / total).astype(jnp.bfloat16)
-        copy = pltpu.make_async_copy(done.at[:, head(number)], out_hbm.at[:, head(number)], load_sem.at[3 + n])
-        copy.start()
-        out_copies.append(copy)
+        out_ref[:, head(number)] = (numerator / total).astype(jnp.bfloat16)
     for copy, goes in sent:
         when(goes, copy.wait_send)
-    for copy in out_copies:
-        copy.wait()
 
 
 MESSAGES = 4 * (ROWS - 1) + 17
@@ -385,9 +377,9 @@
         anywhere = pl.BlockSpec(memory_space=pl.ANY)
         return pl.pallas_call(
             functools.partial(kernel, zs),
-            out_shape=jax.ShapeDtypeStruct(q.shape, jnp.bfloat16),
+            out_shape=pltpu.VMEM(q.shape, jnp.bfloat16),
             in_specs=[anywhere] * 3,
-            out_specs=anywhere,
+            out_specs=pl.BlockSpec(memory_space=pltpu.VMEM),
             scratch_shapes=[
                 pltpu.VMEM((3, BOX, HEADS * BOX), jnp.bfloat16),
                 pltpu.VMEM((3, BOX // 2, HEADS * BOX), jnp.bfloat16),
@@ -402,20 +394,19 @@
                 pltpu.VMEM((2, 5 * BOX // 2, BOX), jnp.bfloat16),
                 pltpu.VMEM((3, 8 * BOX, BOX), jnp.float32),
                 pltpu.VMEM((3, 8 * BOX, BOX), jnp.float32),
-                pltpu.VMEM((ROWS - 1, BOX // 2 + 8, BOX), jnp.float32),
-                pltpu.VMEM((ROWS, BOX // 2 + 8, BOX), jnp.float32),
-                pltpu.VMEM((BOX, HEADS * BOX), jnp.bfloat16),
-                pltpu.SemaphoreType.DMA((3 + HEADS,)),
+                pltpu.VMEM((ROWS - 1, BOX // 2 + 16, BOX), jnp.bfloat16),
+                pltpu.VMEM((ROWS, BOX // 2 + 16, BOX), jnp.bfloat16),
+                pltpu.SemaphoreType.DMA((3,)),
                 pltpu.SemaphoreType.DMA((MESSAGES,)),
                 pltpu.SemaphoreType.DMA((MESSAGES,)),
                 pltpu.SemaphoreType.REGULAR((3,)),
             ],
             compiler_params=pltpu.CompilerParams(
-                collective_id=0, has_side_effects=True, vmem_limit_bytes=60 * 2**20
+                collective_id=0, has_side_effects=True, vmem_limit_bytes=32 * 2**20
             ),
             cost_estimate=pl.CostEstimate(flops=400_000_000, bytes_accessed=2**20, transcendentals=800_000),
             name="attention",
-        )(q, k, v)
+        )(*(pltpu.with_memory_space_constraint(x, pltpu.HBM) for x in (q, k, v)))
 
     spec = P(("doc", "ctx"), None)
     return jax.shard_map(step, mesh=mesh, in_specs=(spec,) * 3, out_specs=spec, check_vma=False)

time: 34.1 us -> 31.5 us (0.924)
  Pallas kernels: 32.3 us -> 30.7 us
  local copies, waits for them, and re-layouts: 1.67 us -> 0.71 us
    pallas_call x1, Pallas kernels: 32.3 us -> 30.7 us  [step(): pl.pallas_call(functools.partial(kernel, zs), out_shape=pltpu.VMEM(q.shap...]
    unnamed x1, local copies, waits for them, and re-layouts: 1.67 us -> 0.71 us
where the time goes in v4:
time: 31.5 us; the launch traced here: 31.4 us
  Pallas kernels  30.7 us (97%)
  local copies, waits for them, and re-layouts  0.71 us (2%)
    pallas_call x1, Pallas kernels, step(): pl.pallas_call(functools.partial(kernel, zs), out_shape=pltpu.VMEM(q.shap...  30.7 us
    unnamed x1, local copies, waits for them, and re-layouts  0.71 us

profile of v4, /device:TPU:121, one launch (start us, length us, event | category | flops | bytes accessed | tf_op | source)
XLA Modules:
  0.0 31.4 jit_solution(9820751682351748189)
XLA Ops:
  0.0 30.7 %attention.1 = bf16[128,1024]{1,0:T(8,128)(2,1)S(1)} custom-call(bf16[128,1024]{1,0:T(8,128)(2,1)} %q_hbm.1, bf16[128,1024]{1,0:T(8,128)(2,1)} %k_hbm.1, bf16[128,1024]{1,0:T(8,128)(2,1)} %v_hbm.1), custom_call_target="tpu_custom_call" | custom-call | flops 400000000 | bytes 1048576 | tf_op jit(solution)/shard_map/attention/pallas_call | solution.py:378
  30.7 0.7 %copy.5 = bf16[128,1024]{1,0:T(8,128)(2,1)} copy(bf16[128,1024]{1,0:T(8,128)(2,1)S(1)} %attention.1) | data formatting | bytes 524288

commit v5 on v4

--- a/solution.py
+++ b/solution.py
@@ -149,6 +149,9 @@
         half1[kind] = pool(source[kind])
         far[kind] = pool(pool(half1[kind]))
     pl.semaphore_wait(barrier, ROWS - 1 + (z + zs - 1) // zs + (2 * zs - 2 - z) // zs)
+
+    upward, downward, everyone = (round_sem.at[n] for n in range(3))
+    when(has_left, lambda: signal(downward, column(z - 1)))
 
     own_third = pl.ds(pl.multiple_of(3 * BOX + rank * third, third), third)
     own_half = pl.ds(pl.multiple_of(2 * BOX + rank * (BOX // 2), BOX // 2), BOX // 2)
@@ -173,56 +176,27 @@
     at_end = (rank == 0) | (rank == ROWS - 1)
     towards = (last == 1) & has_right | (rank == 0) & has_left
     behind = (last == 1) & has_left | (rank == 0) & has_right
-    relay_in = send(source.at[pl.ds(0, 2)], relay, column(z - 1 + 2 * last), towards, behind)
+    beyond = column(z - 1 + 2 * last)
+    before = column(z + 1 - 2 * last)
+    other_end = z * ROWS + ROWS - 1 - rank
+    relay_keys = send(source.at[0], relay.at[0], beyond, towards, behind)
+
+    when(has_left, lambda: pl.semaphore_wait(upward, 1))
+    when(has_right, lambda: signal(upward, column(z + 1)))
+    for other in range(zs // 2):
+        when(z == zs - 1, lambda: signal(everyone, column(other)))
 
     kv3[:, own_third, :] = far[:, :, head(rank)]
     kv1[:, own_half, :] = half1[0:2, :, head(rank)]
     q1[own_query, :] = half1[2, :, head(rank)]
 
-    def tell(turn):
-        reach = 1 << turn
-        when(z >= reach, lambda: signal(round_sem.at[turn], column(z - reach)))
-        when(z < zs - reach, lambda: signal(round_sem.at[turn], column(z + reach)))
-
-    def hear(turn):
-        reach = 1 << turn
-        pl.semaphore_wait(round_sem.at[turn], (z + zs - reach) // zs + (2 * zs - 1 - z - reach) // zs)
-
-    tell(0)
-    hear(0)
-    tell(1)
-    for message in far_in:
-        arrive(message)
-    own3 = kv3.at[:, pl.ds(3 * BOX, BOX), :]
-    a_in = send(own3, kv3.at[:, pl.ds(0, BOX), :], column(z + 2), has_b, has_a)
-    b_in = send(own3, kv3.at[:, pl.ds(BOX, BOX), :], column(z - 2), has_a, has_b)
-    for kind in range(2):
-        kv4[kind, 2 * BOX : 2 * BOX + BOX // 2, :] = pool(kv3[kind, 3 * BOX : 4 * BOX, :])
-    hear(1)
-    tell(2)
-    own4 = kv4.at[:, pl.ds(2 * BOX, BOX // 2), :]
-    half = pl.multiple_of(odd * (BOX // 2), BOX // 2)
-    far4 = [
-        (remote(own4, kv4.at[:, pl.ds(BOX + half, BOX // 2), :], column(mate(mirrored))), has_e),
-        (remote(own4, kv4.at[:, pl.ds(BOX + half, BOX // 2), :], column(mirrored)), has_e),
-        (remote(own4, kv4.at[:, pl.ds(half, BOX // 2), :], column(opposite)), z >= 0),
-        (remote(own4, kv4.at[:, pl.ds(half, BOX // 2), :], column(mate(opposite))), z >= 0),
-    ]
-    sent.extend(far4)
-
-    def send_far4(chosen):
-        when(chosen, lambda: hear(2))
-        for copy, goes in far4:
-            when(chosen & goes, copy.start)
-
-    send_far4(z >= zs // 2)
     near1 = []
-    for turn in (0, 1, 3, 2):
+
+    def send_box1(turn):
         chip = lax.rem(y + turn, 4)
-        back = (4 - turn) % 4
         for flip in range(2):
-            if (back, flip) in kv_in:
-                arrive(kv_in[back, flip])
+            if ((4 - turn) % 4, flip) in kv_in:
+                arrive(kv_in[(4 - turn) % 4, flip])
         up = chip >= 2
         near1.append(
             send(
@@ -233,19 +207,45 @@
                 (up & has_left) | (jnp.logical_not(up) & has_right),
             )
         )
+
+    send_box1(0)
+    when(has_right, lambda: pl.semaphore_wait(downward, 1))
+    for message in far_in:
+        arrive(message)
+    own3 = kv3.at[:, pl.ds(3 * BOX, BOX), :]
+    a_in = send(own3, kv3.at[:, pl.ds(0, BOX), :], column(z + 2), has_b, has_a)
+    b_in = send(own3, kv3.at[:, pl.ds(BOX, BOX), :], column(z - 2), has_a, has_b)
+    for kind in range(2):
+        kv4[kind, 2 * BOX : 2 * BOX + BOX // 2, :] = pool(kv3[kind, 3 * BOX : 4 * BOX, :])
+    own4 = kv4.at[:, pl.ds(2 * BOX, BOX // 2), :]
+    half = pl.multiple_of(odd * (BOX // 2), BOX // 2)
+    far4 = [
+        (remote(own4, kv4.at[:, pl.ds(BOX + half, BOX // 2), :], column(mate(mirrored))), has_e),
+        (remote(own4, kv4.at[:, pl.ds(BOX + half, BOX // 2), :], column(mirrored)), has_e),
+        (remote(own4, kv4.at[:, pl.ds(half, BOX // 2), :], column(opposite)), z >= 0),
+        (remote(own4, kv4.at[:, pl.ds(half, BOX // 2), :], column(mate(opposite))), z >= 0),
+    ]
+    sent.extend(far4)
+
+    def send_far4(chosen):
+        for copy, goes in far4:
+            when(chosen & goes, copy.start)
+
+    send_far4(z >= zs // 2)
+    for turn in (1, 3, 2):
+        send_box1(turn)
     for kind in range(2):
         for n in range(2):
             kv2[kind, (2 + n) * BOX : (3 + n) * BOX, :] = pool(kv1[kind, (2 * n + 2) * BOX : (2 * n + 4) * BOX, :])
     left2 = send(kv2.at[:, pl.ds(2 * BOX, BOX), :], kv2.at[:, pl.ds(0, BOX), :], column(z + 1), has_right, has_left)
     right2 = send(kv2.at[:, pl.ds(3 * BOX, BOX), :], kv2.at[:, pl.ds(5 * BOX, BOX), :], column(z - 1), has_left, has_right)
 
-    send_far4(z < zs // 2)
-
+    relay_values = send(source.at[1], relay.at[1], other_end, towards, behind)
     right0 = send(source.at[pl.ds(0, 2)], near.at[0], me + 1, rank < ROWS - 1, rank > 0)
     left0 = send(source.at[pl.ds(0, 2)], near.at[1], me - 1, rank > 0, rank < ROWS - 1)
-    arrive(relay_in)
-    around0 = send(relay, near.at[1 - last], z * ROWS + ROWS - 1 - rank, behind, towards)
-
+
+    arrive(relay_keys)
+    around_keys = send(relay.at[0], near.at[1 - last, 0], other_end, behind, towards)
     arrive(a_in)
     arrive(b_in)
     c_in = send(
@@ -256,17 +256,23 @@
         has_c,
     )
 
+    when(z < zs // 2, lambda: pl.semaphore_wait(everyone, 1))
+    send_far4(z < zs // 2)
+
     def bias(present):
         return jnp.where(present, 0.0, MASKED).astype(jnp.float32)
 
     left_bias, right_bias = bias(has_left), bias(has_right)
 
+    arrive(relay_values)
+    around_values = send(relay.at[1], near.at[last, 1], before, behind, towards)
     for message in q_in:
         arrive(message)
     for n in range(2):
         q2[n * BOX : (n + 1) * BOX, :] = pool(q1[2 * n * BOX : (2 * n + 2) * BOX, :])
     q3 = pool(q2[...])
     q4 = pool(q3)
+
 
     def box(ref, kind, start):
         return ref[kind, start * BOX : (start + 1) * BOX, :]
@@ -337,7 +343,8 @@
 
     arrive(right0)
     arrive(left0)
-    arrive(around0)
+    arrive(around_keys)
+    arrive(around_values)
     start_bias, end_bias = bias(jnp.logical_not(starts)), bias(jnp.logical_not(ends))
     for n in range(HEADS):
         columns = slice(n * BOX, (n + 1) * BOX)
@@ -367,7 +374,7 @@
         when(goes, copy.wait_send)
 
 
-MESSAGES = 4 * (ROWS - 1) + 17
+MESSAGES = 4 * (ROWS - 1) + 19
 
 
 def solution(mesh):

time: 31.5 us -> 29.9 us (0.949)
  the two profiles are of different devices: /device:TPU:121 before, /device:TPU:101 now
where the time goes in v5:
time: 29.9 us; the launch traced here: 29.8 us
  Pallas kernels  29.1 us (97%)
  local copies, waits for them, and re-layouts  0.71 us (2%)
    pallas_call x1, Pallas kernels, step(): pl.pallas_call(functools.partial(kernel, zs), out_shape=pltpu.VMEM(q.shap...  29.1 us
    unnamed x1, local copies, waits for them, and re-layouts  0.71 us

profile of v5, /device:TPU:101, one launch (start us, length us, event | category | flops | bytes accessed | tf_op | source)
XLA Modules:
  0.0 29.8 jit_solution(2066309941805393447)
XLA Ops:
  0.0 29.1 %attention.1 = bf16[128,1024]{1,0:T(8,128)(2,1)S(1)} custom-call(bf16[128,1024]{1,0:T(8,128)(2,1)} %q_hbm.1, bf16[128,1024]{1,0:T(8,128)(2,1)} %k_hbm.1, bf16[128,1024]{1,0:T(8,128)(2,1)} %v_hbm.1), custom_call_target="tpu_custom_call" | custom-call | flops 400000000 | bytes 1048576 | tf_op jit(solution)/shard_map/attention/pallas_call | solution.py:385
  29.1 0.7 %copy.5 = bf16[128,1024]{1,0:T(8,128)(2,1)} copy(bf16[128,1024]{1,0:T(8,128)(2,1)S(1)} %attention.1) | data formatting | bytes 524288

commit v6 on v5

--- a/solution.py
+++ b/solution.py
@@ -62,6 +62,7 @@
 
     peers = [(2, 0), (2, 1), (1, 0), (1, 1), (3, 0), (3, 1), (0, 1)]
     opposite = lax.rem(z + zs // 2, zs)
+    passed_on = (z == zs // 4) | (z == zs // 4 + 1)
     mirrored = zs - 1 - z
     has_left = z > 0
     has_right = z < zs - 1
@@ -222,7 +223,7 @@
     far4 = [
         (remote(own4, kv4.at[:, pl.ds(BOX + half, BOX // 2), :], column(mate(mirrored))), has_e),
         (remote(own4, kv4.at[:, pl.ds(BOX + half, BOX // 2), :], column(mirrored)), has_e),
-        (remote(own4, kv4.at[:, pl.ds(half, BOX // 2), :], column(opposite)), z >= 0),
+        (remote(own4, kv4.at[:, pl.ds(half, BOX // 2), :], column(opposite)), z < zs - 2),
         (remote(own4, kv4.at[:, pl.ds(half, BOX // 2), :], column(mate(opposite))), z >= 0),
     ]
     sent.extend(far4)
@@ -301,6 +302,15 @@
     for n, boxes in enumerate(((0, 4, 5), (1, 5, 0), (2, 6, 7), (3, 7, 2))):
         biases = [left_bias if b < 2 else right_bias if b >= 6 else None for b in boxes]
         level1.append(raised(level(q1[n * BOX : (n + 1) * BOX, :], kv1, boxes, biases), 1))
+    arrive(far4[0])
+    passed = send(
+        kv4.at[:, pl.ds(pl.multiple_of(BOX + half, BOX // 2), BOX // 2), :],
+        kv4.at[:, pl.ds(half, BOX // 2), :],
+        column(z + 2),
+        z < 2,
+        passed_on,
+    )
+
     arrive(left2)
     arrive(right2)
     for n, boxes in enumerate(((0, 4, 5), (1, 5, 0))):
@@ -314,8 +324,10 @@
 
     arrive(c_in)
     level3 = raised(level(q3, kv3, (0, 1, 2), [bias(has_a), bias(has_b), bias(has_c)]), 3)
-    for message in far4:
-        arrive(message)
+    arrive(far4[1])
+    when(jnp.logical_not(passed_on), far4[2][0].wait_recv)
+    arrive(passed)
+    arrive(far4[3])
     repeated(raised(level(q4, kv4, (0, 1), [None, bias(has_e)]), 4), 0, 2)
     repeated(merge(level3, risen(0, BOX)), 4 * BOX, 4)
 
@@ -374,7 +386,7 @@
         when(goes, copy.wait_send)
 
 
-MESSAGES = 4 * (ROWS - 1) + 19
+MESSAGES = 4 * (ROWS - 1) + 20
 
 
 def solution(mesh):

time: 29.9 us -> 29.2 us (0.977)
  Pallas kernels: 29.1 us -> 28.4 us
    pallas_call x1, Pallas kernels: 29.1 us -> 28.4 us  [step(): pl.pallas_call(functools.partial(kernel, zs), out_shape=pltpu.VMEM(q.shap...]
where the time goes in v6:
time: 29.2 us; the launch traced here: 29.1 us
  Pallas kernels  28.4 us (97%)
  local copies, waits for them, and re-layouts  0.71 us (2%)
    pallas_call x1, Pallas kernels, step(): pl.pallas_call(functools.partial(kernel, zs), out_shape=pltpu.VMEM(q.shap...  28.4 us
    unnamed x1, local copies, waits for them, and re-layouts  0.71 us

profile of v6, /device:TPU:101, one launch (start us, length us, event | category | flops | bytes accessed | tf_op | source)
XLA Modules:
  0.0 29.1 jit_solution(3369358177768501292)
XLA Ops:
  0.0 28.4 %attention.1 = bf16[128,1024]{1,0:T(8,128)(2,1)S(1)} custom-call(bf16[128,1024]{1,0:T(8,128)(2,1)} %q_hbm.1, bf16[128,1024]{1,0:T(8,128)(2,1)} %k_hbm.1, bf16[128,1024]{1,0:T(8,128)(2,1)} %v_hbm.1), custom_call_target="tpu_custom_call" | custom-call | flops 400000000 | bytes 1048576 | tf_op jit(solution)/shard_map/attention/pallas_call | solution.py:397
  28.4 0.7 %copy.5 = bf16[128,1024]{1,0:T(8,128)(2,1)} copy(bf16[128,1024]{1,0:T(8,128)(2,1)S(1)} %attention.1) | data formatting | bytes 524288

commit v7 on v6

--- a/solution.py
+++ b/solution.py
@@ -24,17 +24,26 @@
     return jnp.dot(pairs, rows, preferred_element_type=jnp.float32).astype(jnp.bfloat16)
 
 
-def attend(query, keys, values, biases):
+def attend(units):
     scores = []
-    for key, bias in zip(keys, biases):
-        score = lax.dot_general(query, key, (((1,), (1,)), ((), ())), preferred_element_type=jnp.float32) * TO_LOG2
-        scores.append(score if bias is None else score + bias)
-    peak = jnp.max(functools.reduce(jnp.maximum, scores), axis=1, keepdims=True)
-    shifted = [jnp.exp2(score - peak) for score in scores]
-    total = jnp.sum(functools.reduce(jnp.add, shifted), axis=1, keepdims=True)
-    weights = jnp.concatenate([part.astype(jnp.bfloat16) for part in shifted], axis=1)
-    numerator = jnp.dot(weights, jnp.concatenate(values, axis=0), preferred_element_type=jnp.float32)
-    return jnp.broadcast_to(peak, numerator.shape), jnp.broadcast_to(total, numerator.shape), numerator
+    for query, keys, _, biases in units:
+        parts = []
+        for key, bias in zip(keys, biases):
+            score = lax.dot_general(query, key, (((1,), (1,)), ((), ())), preferred_element_type=jnp.float32) * TO_LOG2
+            parts.append(score if bias is None else score + bias)
+        scores.append(parts)
+    peaks = [jnp.max(functools.reduce(jnp.maximum, parts), axis=1, keepdims=True) for parts in scores]
+    shifted = [[jnp.exp2(part - peak) for part in parts] for parts, peak in zip(scores, peaks)]
+    totals = [jnp.sum(functools.reduce(jnp.add, parts), axis=1, keepdims=True) for parts in shifted]
+    weights = [jnp.concatenate([part.astype(jnp.bfloat16) for part in parts], axis=1) for parts in shifted]
+    numerators = [
+        jnp.dot(weight, jnp.concatenate(unit[2], axis=0), preferred_element_type=jnp.float32)
+        for weight, unit in zip(weights, units)
+    ]
+    return [
+        (jnp.broadcast_to(peak, numerator.shape), jnp.broadcast_to(total, numerator.shape), numerator)
+        for peak, total, numerator in zip(peaks, totals, numerators)
+    ]
 
 
 def merge(one, other):
@@ -278,8 +287,8 @@
     def box(ref, kind, start):
         return ref[kind, start * BOX : (start + 1) * BOX, :]
 
-    def level(query, ref, boxes, biases):
-        return attend(query, [box(ref, 0, b) for b in boxes], [box(ref, 1, b) for b in boxes], biases)
+    def unit(query, ref, boxes, biases):
+        return query, [box(ref, 0, b) for b in boxes], [box(ref, 1, b) for b in boxes], biases
 
     def raised(values, height):
         return values[0] + float(height), values[1], values[2]
@@ -298,10 +307,11 @@
     for kind in range(2):
         kv2[kind, BOX : 2 * BOX, :] = pool(kv1[kind, 0 : 2 * BOX, :])
         kv2[kind, 4 * BOX : 5 * BOX, :] = pool(kv1[kind, 6 * BOX : 8 * BOX, :])
-    level1 = []
+    units = []
     for n, boxes in enumerate(((0, 4, 5), (1, 5, 0), (2, 6, 7), (3, 7, 2))):
         biases = [left_bias if b < 2 else right_bias if b >= 6 else None for b in boxes]
-        level1.append(raised(level(q1[n * BOX : (n + 1) * BOX, :], kv1, boxes, biases), 1))
+        units.append(unit(q1[n * BOX : (n + 1) * BOX, :], kv1, boxes, biases))
+    level1 = [raised(values, 1) for values in attend(units)]
     arrive(far4[0])
     passed = send(
         kv4.at[:, pl.ds(pl.multiple_of(BOX + half, BOX // 2), BOX // 2), :],
@@ -313,22 +323,24 @@
 
     arrive(left2)
     arrive(right2)
+    units = []
     for n, boxes in enumerate(((0, 4, 5), (1, 5, 0))):
         biases = [left_bias if b < 2 else right_bias for b in boxes]
-        level2 = raised(level(q2[n * BOX : (n + 1) * BOX, :], kv2, boxes, biases), 2)
-        repeated(level2, 2 * n * BOX, 2)
+        units.append(unit(q2[n * BOX : (n + 1) * BOX, :], kv2, boxes, biases))
+    for n, values in enumerate(attend(units)):
+        repeated(raised(values, 2), 2 * n * BOX, 2)
         for m in range(2):
             merged = merge(level1[2 * n + m], risen((2 * n + m) * BOX, BOX))
             for kind in range(3):
                 terms[kind, (2 * n + m) * BOX : (2 * n + m + 1) * BOX, :] = merged[kind]
 
     arrive(c_in)
-    level3 = raised(level(q3, kv3, (0, 1, 2), [bias(has_a), bias(has_b), bias(has_c)]), 3)
+    level3 = raised(attend([unit(q3, kv3, (0, 1, 2), [bias(has_a), bias(has_b), bias(has_c)])])[0], 3)
     arrive(far4[1])
     when(jnp.logical_not(passed_on), far4[2][0].wait_recv)
     arrive(passed)
     arrive(far4[3])
-    repeated(raised(level(q4, kv4, (0, 1), [None, bias(has_e)]), 4), 0, 2)
+    repeated(raised(attend([unit(q4, kv4, (0, 1), [None, bias(has_e)])])[0], 4), 0, 2)
     repeated(merge(level3, risen(0, BOX)), 4 * BOX, 4)
 
     here = lax.broadcasted_iota(jnp.int32, (BOX // 2, BOX), 0) == lax.broadcasted_iota(jnp.int32, (BOX // 2, BOX), 1)
@@ -358,16 +370,21 @@
     arrive(around_keys)
     arrive(around_values)
     start_bias, end_bias = bias(jnp.logical_not(starts)), bias(jnp.logical_not(ends))
-    for n in range(HEADS):
-        columns = slice(n * BOX, (n + 1) * BOX)
-        values = attend(
-            source[2, :, columns],
-            [near[0, 0, :, columns], source[0, :, columns], near[1, 0, :, columns]],
-            [near[0, 1, :, columns], source[1, :, columns], near[1, 1, :, columns]],
-            [start_bias, None, end_bias],
-        )
-        for kind in range(3):
-            terms[kind, n * BOX : (n + 1) * BOX, :] = values[kind]
+    for first in range(0, HEADS, 4):
+        units = []
+        for n in range(first, first + 4):
+            columns = slice(n * BOX, (n + 1) * BOX)
+            units.append(
+                (
+                    source[2, :, columns],
+                    [near[0, 0, :, columns], source[0, :, columns], near[1, 0, :, columns]],
+                    [near[0, 1, :, columns], source[1, :, columns], near[1, 1, :, columns]],
+                    [start_bias, None, end_bias],
+                )
+            )
+        for n, values in enumerate(attend(units), first):
+            for kind in range(3):
+                terms[kind, n * BOX : (n + 1) * BOX, :] = values[kind]
 
     for n, (turn, flip) in enumerate([(0, 0)] + peers[::-1]):
         if n:

time: 29.2 us -> 28.6 us (0.979)
  Pallas kernels: 28.4 us -> 27.7 us
    pallas_call x1, Pallas kernels: 28.4 us -> 27.7 us  [step(): pl.pallas_call(functools.partial(kernel, zs), out_shape=pltpu.VMEM(q.shap...]
where the time goes in v7:
time: 28.6 us; the launch traced here: 28.4 us
  Pallas kernels  27.7 us (97%)
  local copies, waits for them, and re-layouts  0.71 us (2%)
    pallas_call x1, Pallas kernels, step(): pl.pallas_call(functools.partial(kernel, zs), out_shape=pltpu.VMEM(q.shap...  27.7 us
    unnamed x1, local copies, waits for them, and re-layouts  0.71 us

profile of v7, /device:TPU:101, one launch (start us, length us, event | category | flops | bytes accessed | tf_op | source)
XLA Modules:
  0.0 28.4 jit_solution(1183557714267622019)
XLA Ops:
  0.0 27.7 %attention.1 = bf16[128,1024]{1,0:T(8,128)(2,1)S(1)} custom-call(bf16[128,1024]{1,0:T(8,128)(2,1)} %q_hbm.1, bf16[128,1024]{1,0:T(8,128)(2,1)} %k_hbm.1, bf16[128,1024]{1,0:T(8,128)(2,1)} %v_hbm.1), custom_call_target="tpu_custom_call" | custom-call | flops 400000000 | bytes 1048576 | tf_op jit(solution)/shard_map/attention/pallas_call | solution.py:414
  27.7 0.7 %copy.5 = bf16[128,1024]{1,0:T(8,128)(2,1)} copy(bf16[128,1024]{1,0:T(8,128)(2,1)S(1)} %attention.1) | data formatting | bytes 524288

commit v8 on v7

--- a/solution.py
+++ b/solution.py
@@ -132,6 +132,9 @@
     def remote(src, dst, device):
         number = used[0]
         used[0] += 1
+        return way(number, src, dst, device)
+
+    def way(number, src, dst, device):
         return pltpu.make_async_remote_copy(
             src_ref=src,
             dst_ref=dst,
@@ -359,11 +362,22 @@
         parts = jnp.where(line == 0, high, jnp.where(line == 1, middle, weight - high - middle))
         box_out[BOX // 2 :, :] = jnp.where(line < 3, parts, 0.0).astype(jnp.bfloat16)
 
-    home = {}
-    for n, (turn, flip) in enumerate(peers):
-        finish(ring(turn, flip), parcel.at[n])
-        home[turn, flip] = send(parcel.at[n], inbox.at[rank], z * ROWS + ring(turn, flip))
-    finish(rank, inbox.at[rank])
+    first = used[0]
+    used[0] += ROWS - 1
+    for number in range(ROWS):
+        turn, flip = lax.rem(number // 2 + 4 - y, 4), lax.rem(number % 2 + core, 2)
+        finish(number, parcel.at[number])
+
+        @pl.when(number != rank)
+        def _():
+            way(first + 2 * turn + flip - 1, parcel.at[number], inbox.at[rank], z * ROWS + number).start()
+
+    inbox[rank] = parcel[rank]
+    home = {
+        (turn, flip): (way(first + 2 * turn + flip - 1, parcel.at[0], inbox.at[rank], z * ROWS + ring(turn, flip)), None)
+        for turn, flip in peers
+    }
+    sent.extend(home.values())
 
     arrive(right0)
     arrive(left0)
@@ -430,7 +444,7 @@
                 pltpu.VMEM((2, 5 * BOX // 2, BOX), jnp.bfloat16),
                 pltpu.VMEM((3, 8 * BOX, BOX), jnp.float32),
                 pltpu.VMEM((3, 8 * BOX, BOX), jnp.float32),
-                pltpu.VMEM((ROWS - 1, BOX // 2 + 16, BOX), jnp.bfloat16),
+                pltpu.VMEM((ROWS, BOX // 2 + 16, BOX), jnp.bfloat16),
                 pltpu.VMEM((ROWS, BOX // 2 + 16, BOX), jnp.bfloat16),
                 pltpu.SemaphoreType.DMA((3,)),
                 pltpu.SemaphoreType.DMA((MESSAGES,)),

time: 28.6 us -> 28.3 us (0.990)
  no operation moved by 1% of the time
where the time goes in v8:
time: 28.3 us; the launch traced here: 28.2 us
  Pallas kernels  27.5 us (97%)
  local copies, waits for them, and re-layouts  0.71 us (3%)
    pallas_call x1, Pallas kernels, step(): pl.pallas_call(functools.partial(kernel, zs), out_shape=pltpu.VMEM(q.shap...  27.5 us
    unnamed x1, local copies, waits for them, and re-layouts  0.71 us

profile of v8, /device:TPU:101, one launch (start us, length us, event | category | flops | bytes accessed | tf_op | source)
XLA Modules:
  0.0 28.2 jit_solution(8986476384671420656)
XLA Ops:
  0.0 27.5 %attention.1 = bf16[128,1024]{1,0:T(8,128)(2,1)S(1)} custom-call(bf16[128,1024]{1,0:T(8,128)(2,1)} %q_hbm.1, bf16[128,1024]{1,0:T(8,128)(2,1)} %k_hbm.1, bf16[128,1024]{1,0:T(8,128)(2,1)} %v_hbm.1), custom_call_target="tpu_custom_call" | custom-call | flops 400000000 | bytes 1048576 | tf_op jit(solution)/shard_map/attention/pallas_call | solution.py:428
  27.5 0.7 %copy.5 = bf16[128,1024]{1,0:T(8,128)(2,1)} copy(bf16[128,1024]{1,0:T(8,128)(2,1)S(1)} %attention.1) | data formatting | bytes 524288
